TPU v7x, 512 devices: a whole 4x4x16 slice. The times are simulated.
512 devices in a mesh: shard: 32 (over z, core), grp: 16 (over y, x).
Axes of the slice: x: 4, y: 4, z: 16, core: 2. Of those that a mesh axis runs over, the one named last changes fastest.
Arguments:
- embeddings: bfloat16 [65536, 4096], P(('shard', 'grp')), parts along dimension 0, as said below
- cluster_ids: int32 [65536], P(('shard', 'grp')), parts along dimension 0, may hold values from 0 to 2047, as said below
- order: int32 [65536], P(('shard', 'grp')), parts along dimension 0, may hold values from 0 to 2047, each once
Outputs:
- best: float32 [65536], P(('shard', 'grp')), parts along dimension 0
There are 32 independent parts, one for each index of `shard`. A program takes and returns all parts, laid end to end along the dimension named above; each array names one. Nothing has to cross between parts.
Inputs may be any that keep to these rules, and one draw needn't show every extreme that they name: `cluster_ids`: never falling along the rows, so each cluster is a run of consecutive rows; a cluster's id is the index of its last row. Exactly one cluster has 1024 rows, every other has 1 to 96. `embeddings`: every row is nonzero.
All inputs are finite; a program needn't handle non-finite values.
Results may differ from a plain program's by a relative error of at most 0.0009.
Values may be sent and summed in bfloat16 or wider, within the bound.
No kernel may reach another device: no remote copies, remote signals or barrier semaphores. Data moves between devices by JAX's collectives and lax.ppermute only.
A program may use at most 64 MiB of HBM per device.

v0:
```python
import jax
import jax.numpy as jnp
from jax import lax
from jax.sharding import PartitionSpec as P


def similar(left, right):
    return lax.dot_general(
        left, right, (((1,), (1,)), ((), ())), preferred_element_type=jnp.float32
    )


def normalize(embeddings):
    wide = embeddings.astype(jnp.float32)
    squares = jnp.sum(wide * wide, axis=1, keepdims=True)
    return (wide * lax.rsqrt(squares + 1e-06)).astype(jnp.bfloat16)


def body(embeddings, cluster_ids, order):
    rows = embeddings.shape[0]
    unit = normalize(embeddings)
    all_ids, all_order = (
        lax.all_gather(cluster_ids, "grp", axis=0, tiled=True),
        lax.all_gather(order, "grp", axis=0, tiled=True),
    )
    lowest = jnp.full((rows,), -1.0, jnp.float32)
    piece = lax.all_gather(unit, "grp", axis=0, tiled=True)

    def work(value):
        scores = similar(unit, piece)
        keep = (cluster_ids[:, None] == all_ids[None, :]) & (all_order[None, :] < order[:, None])
        return jnp.maximum(value, jnp.max(jnp.where(keep, scores, -1.0), axis=1))

    touch = (all_ids[0] <= cluster_ids[-1]) & (cluster_ids[0] <= all_ids[-1])
    return lax.cond(touch, work, lambda value: value, lowest)


def solution(mesh):
    return jax.shard_map(
        body,
        mesh=mesh,
        in_specs=(P(("shard", "grp"), None), P(("shard", "grp")), P(("shard", "grp"))),
        out_specs=P(("shard", "grp")),
        check_vma=False,
    )
```

profile of v0, /device:TPU:1, one launch (start us, length us, event | category | flops | bytes accessed | tf_op | source)
XLA Modules:
  0.0 161.8 jit_solution(11042394266655661974)
XLA Ops:
  6.5 0.0 copy-start
  6.5 0.0 copy-start.1
  6.5 0.0 all-gather.4.cloned.1.call-start
  6.5 1.5 fusion.1
  8.1 2.5 %fusion.2 = bf16[128,4096]{1,0:T(8,128)(2,1)} fusion(bf16[128,4096]{1,0:T(8,128)(2,1)} %param.5, f32[128]{0:T(128)S(1)} %add_rsqrt_fusion), kind=kLoop, calls=%fused_computation.6 | loop fusion | flops 1572864 | bytes 2097664 | tf_op jit(solution)/shard_map/convert_element_type | solution.py:16
  10.5 0.0 all-gather.4.cloned.1.call-update
  10.6 0.0 copy-done
  10.6 17.3 %all-gather = s32[16,1,128]{2,1,0:T(1,128)S(1)} all-gather(s32[1,1,128]{2,1,0:T(1,128)S(1)} %bitcast.10), channel_id=1, replica_groups=mesh['shard'=32,'grp'=16] {'grp'}, dimensions={0}, use_global_device_ids=true | all-gather | bytes 8704 | tf_op jit(solution)/shard_map/all_gather | solution.py:23
  27.9 0.6 fusion.4
  28.5 0.6 fusion.3
  31.6 0.0 copy-done.1
  31.6 16.0 %all-gather.1 = s32[16,1,128]{2,1,0:T(1,128)S(1)} all-gather(s32[1,1,128]{2,1,0:T(1,128)S(1)} %bitcast.11), channel_id=1, replica_groups=mesh['shard'=32,'grp'=16] {'grp'}, dimensions={0}, use_global_device_ids=true | all-gather | bytes 8704 | tf_op jit(solution)/shard_map/all_gather | solution.py:24
  47.5 95.1 %all-gather.4.cloned.1.call-done = bf16[2048,4096]{1,0:T(8,128)(2,1)} async-done(((bf16[128,4096]{1,0:T(8,128)(2,1)}), bf16[2048,4096]{1,0:T(8,128)(2,1)}) %all-gather.4.cloned.1.call-update) | async-done | bytes 16777232 | tf_op jit(solution)/shard_map/all_gather | solution.py:27
  142.6 11.9 %conditional.1 = (f32[128]{0:T(128)S(1)}) conditional(s32[]{:T(128)} %bitcast.2, () %tuple.11, (s32[128]{0:T(128)S(1)}, s32[2048]{0:T(1024)S(1)}, s32[2048]{0:T(1024)S(1)}, s32[128]{0:T(128)S(1)}, bf16[128,4096]{1,0:T(8,128)(2,1)}, /*index=5*/bf16[2048,4096]{1,0:T(8,128)(2,1)}) %tuple.24), branch_computations={%region_1.0_spmd, %region_2.4_spmd} | conditional | flops 2148794368 | bytes 17844744 | solution.py:35
  142.6 11.8 %fusion = f32[128]{0:T(128)S(1)} fusion(bf16[128,4096]{1,0:T(8,128)(2,1)} %get-tuple-element.24, bf16[2048,4096]{1,0:T(8,128)(2,1)} %get-tuple-element.25, s32[2048]{0:T(1024)S(1)} %get-tuple-element.22, s32[2048]{0:T(1024)S(1)} %get-tuple-element.21, s32[128]{0:T(128)S(1)} %get-tuple-element.23, s32[128]{0:T(128)S(1)} %get-tuple-element.20), kind=kOutput, calls=%fused_computation.1 | convolution fusion | flops 2148794368 | bytes 17843712 | tf_op jit(solution)/shard_map/cond/branch_1_fun/dot_general | solution.py:8
  154.5 0.0 copy-start.2
  154.5 0.5 copy-done.2
  (2 shorter events, 0.0 us)
Async XLA Ops:
  6.5 4.0 %copy-start = (s32[128]{0:T(128)S(1)}, s32[128]{0:T(128)}, u32[]{:S(2)}) copy-start(s32[128]{0:T(128)} %param.6) | copy-start | bytes 1540
  6.5 25.0 %copy-start.1 = (s32[128]{0:T(128)S(1)}, s32[128]{0:T(128)}, u32[]{:S(2)}) copy-start(s32[128]{0:T(128)} %param.7) | copy-start | bytes 1540
  6.5 136.1 %all-gather.4.cloned.1.call-start = ((), (), s32[]{:S(2)}) async-start(), calls=%async_computation | async-start | bytes 17825792 | tf_op jit(solution)/shard_map/all_gather | solution.py:27
  154.5 0.5 copy-start.2
Sparse Core Ops, SparseCore 0:
  10.7 131.8 all-gather.3
where the time goes:
time: 162 us
  waiting for transfers between devices  95.1 us (59%)
  blocking collectives  33.3 us (21%)
  between operations  15.9 us (10%)
  matrix products  11.8 us (7%)
  other arithmetic  4.01 us (2%)
  local copies, waits for them, and re-layouts  1.7 us (1%)
    all_gather x1, waiting for transfers between devices, body(): piece = lax.all_gather(unit, 'grp', axis=0, tiled=True)  95.1 us
    all_gather x1, blocking collectives, body(): lax.all_gather(cluster_ids, 'grp', axis=0, tiled=True)  17.3 us
    all_gather x1, blocking collectives, body(): lax.all_gather(order, 'grp', axis=0, tiled=True)  16 us
    dot_general x1, matrix products, similar(): lax.dot_general(left, right, (((1,), (1,)), ((), ())), preferred_element_...  11.8 us
  transfers between devices with their start and end apart: 1, of which 1 were waited for; matrix products, arithmetic and copies ran while one was open for 1% of the time, Pallas kernels for 0%

commit v1 on v0

v1 whole, which is shorter than its diff:
```python
import jax
import jax.numpy as jnp
from jax import lax
from jax.experimental import pallas as pl
from jax.experimental.pallas import tpu as pltpu
from jax.sharding import PartitionSpec as P

HALF = 64
EDGE = 96
META = 128
BIG = 1024

FETCH = (
    (3, 8, 14, 15, 7, 1, 11, 4, 9, 5, 6, 10, 0, 12, 13, 2),
    (12, 5, 3, 6, 1, 10, 2, 13, 7, 4, 14, 8, 11, 0, 15, 9),
    (5, 6, 1, 4, 0, 8, 7, 11, 12, 13, 9, 14, 15, 2, 10, 3),
    (15, 13, 10, 2, 6, 4, 5, 3, 11, 14, 12, 7, 1, 9, 0, 8),
)


def dot_nt(left, right):
    return lax.dot_general(left, right, (((1,), (1,)), ((), ())), preferred_element_type=jnp.float32)


def unit_rows(raw):
    wide = raw.astype(jnp.float32)
    squares = jnp.sum(wide * wide, axis=1, keepdims=True)
    return (wide * lax.rsqrt(squares + 1e-06)).astype(jnp.bfloat16)


def pair_form(first, lanes=META):
    a = lax.broadcasted_iota(jnp.int32, (lanes, lanes), 0)
    b = lax.broadcasted_iota(jnp.int32, (lanes, lanes), 1)
    plus = ((a == first) & (b == 2)) | ((a == first + 1) & (b == 3))
    minus = ((a == 2) & (b == first)) | ((a == 3) & (b == first + 1))
    return jnp.where(plus, 1.0, jnp.where(minus, -1.0, 0.0)).astype(jnp.bfloat16)


def difference(meta, first):
    left = jnp.dot(meta, pair_form(first), preferred_element_type=jnp.float32).astype(jnp.bfloat16)
    return dot_nt(left, meta)


def pack_kernel(place, emb, ids, order, msg, edge, meta_out):
    me, core = place[0], place[1]
    width = emb.shape[1]
    rows = emb.shape[0]
    row = lax.broadcasted_iota(jnp.int32, (8, rows), 0)
    lane = lax.broadcasted_iota(jnp.int32, (8, rows), 1)
    id_all = jnp.broadcast_to(ids[...], (8, rows))
    order_all = jnp.broadcast_to(order[...], (8, rows))
    far = jnp.where(id_all - (me * rows + lane) >= EDGE, id_all + 1, 0)
    far = jnp.broadcast_to(jnp.max(far, axis=1, keepdims=True), (8, rows))
    value = jnp.where(row < 2, order_all, jnp.where(row < 6, id_all, far))
    low = value & 127
    parts = jnp.where((row & 1) == 0, value - low, low)
    parts = jnp.where((row == 2) | (row == 3), 1, parts).astype(jnp.float32)
    wide = jnp.concatenate([parts, jnp.zeros((META - 8, rows), jnp.float32)], axis=0)
    meta = wide.T.astype(jnp.bfloat16)
    meta_out[...] = meta
    start = pl.multiple_of(jnp.where(me < 8, HALF, 0), HALF)
    msg[:, :width] = emb[pl.ds(start, HALF), :]
    msg[:, width:] = meta_out[pl.ds(start, HALF), :]
    begin = pl.multiple_of(jnp.where(core == 0, rows - EDGE, 0), 32)
    edge[:, :width] = emb[pl.ds(begin, EDGE), :]
    edge[:, width:] = meta_out[pl.ds(begin, EDGE), :]


def column(meta, first):
    return meta[:, first : first + 1] + meta[:, first + 1 : first + 2]


def merge_kernel(place, own, own_meta, msg, out):
    me = place[0]
    width = own.shape[1]
    rows = 2 * HALF
    is_low = me < 8
    start = pl.multiple_of(jnp.where(is_low, 0, HALF), HALF)
    mine_first = own_meta[0:8, :].astype(jnp.float32)[0:1]
    theirs_first = msg[0:8, width:].astype(jnp.float32)[0:1]
    low_first = jnp.where(is_low, mine_first, theirs_first)
    high_first = jnp.where(is_low, theirs_first, mine_first)
    far = column(low_first, 6)
    last = jnp.where(far > 0, far - 1, column(high_first, 4))
    slot = (me & 7) * rows + jnp.where(is_low, 0, HALF) + lax.broadcasted_iota(jnp.int32, (HALF, 1), 0)
    low_row = (slot.astype(jnp.float32) >= last - (BIG - 1)).astype(jnp.float32)
    take = jnp.where(is_low, low_row, 1.0 - low_row) > 0.5
    raw = jnp.where(take, own[...].astype(jnp.float32), msg[:, :width].astype(jnp.float32))
    squares = jnp.sum(raw * raw, axis=1, keepdims=True)
    out[:, :width] = (raw * lax.rsqrt(squares + 1e-06)).astype(jnp.bfloat16)
    mine = own_meta[pl.ds(start, HALF), :].astype(jnp.float32)
    meta = jnp.where(take, mine, msg[:, width:].astype(jnp.float32))
    lane = lax.broadcasted_iota(jnp.int32, (HALF, META), 1)
    high = jnp.floor(last * (1.0 / 128)) * 128
    meta = jnp.where(lane == 6, high, jnp.where(lane == 7, last - high, meta))
    out[:, width:] = meta.astype(jnp.bfloat16)


def near_kernel(emb, own_meta, edge, msg, best, unit, meta):
    width = emb.shape[1]
    rows = emb.shape[0]
    for ref, begin, count in ((emb, 0, rows), (edge, rows, EDGE), (msg, rows + EDGE, HALF)):
        for at in range(0, count, 32):
            unit[begin + at : begin + at + 32, :] = unit_rows(ref[at : at + 32, :width])
    meta[0:rows, :] = own_meta[...]
    meta[rows : rows + EDGE, :] = edge[:, width:]
    meta[rows + EDGE :, :] = msg[:, width:]
    total = rows + EDGE + HALF
    scores = dot_nt(unit[...], unit[...])
    keep = (difference(meta[...], 4) == 0) & (difference(meta[...], 0) < 0)
    found = jnp.max(jnp.where(keep, scores, -1.0), axis=0, keepdims=True)
    best[...] = jnp.broadcast_to(found, (8, total))


def far_kernel(place, *refs):
    blocks, metas, (near, out, scores) = refs[:5], refs[5:10], refs[10:]
    step = pl.program_id(0)
    rows = 2 * HALF
    part = jnp.concatenate([b[...] for b in blocks], axis=0)
    product = dot_nt(part, part)

    @pl.when(step == 0)
    def _():
        scores[...] = product

    @pl.when(step > 0)
    def _():
        scores[...] += product

    @pl.when(step == pl.num_programs(0) - 1)
    def _():
        me, core = place[0], place[1]
        meta = jnp.concatenate([m[...] for m in metas], axis=0)
        keep = difference(meta, 0) < 0
        found = jnp.max(jnp.where(keep, scores[...], -1.0), axis=0, keepdims=True)
        dest = lax.broadcasted_iota(jnp.int32, (16, rows), 0)
        lane = lax.broadcasted_iota(jnp.int32, (16, rows), 1)
        last = column(metas[0][0:8, :].astype(jnp.float32)[0:1], 6).astype(jnp.int32)
        at = dest * rows + lane
        inside = (at <= last) & (at > last - BIG)
        total = jnp.full((16, rows), -1.0, jnp.float32)
        for k in range(5):
            group = place[2 + k]
            piece = found[:, k * HALF : (k + 1) * HALF]
            both = jnp.concatenate([piece, piece], axis=1)
            here = inside & ((dest & 7) == (group & 7)) & ((lane >= HALF) == (group >= 8))
            total = jnp.maximum(total, jnp.where(here, both, -1.0))
        none = jnp.full((1, rows - EDGE), -1.0, jnp.float32)
        own = near[0:1, 0:rows]
        side = near[0:1, rows : rows + EDGE]
        other = near[0:1, rows + EDGE :]
        total = jnp.maximum(total, jnp.where(dest == me, own, -1.0))
        before = jnp.concatenate([none, side], axis=1)
        after = jnp.concatenate([side, none], axis=1)
        total = jnp.maximum(total, jnp.where((core == 0) & (dest == ((me + 15) & 15)), before, -1.0))
        total = jnp.maximum(total, jnp.where((core == 1) & (dest == ((me + 1) & 15)), after, -1.0))
        there = (dest == (me ^ 8)) & ((lane >= HALF) == (me >= 8))
        total = jnp.maximum(total, jnp.where(there, jnp.concatenate([other, other], axis=1), -1.0))
        out[...] = total


def solution(mesh):
    n_shard, n_grp = mesh.shape["shard"], mesh.shape["grp"]
    axes = ("shard", "grp")

    def swap(pairs_of):
        return [(s * n_grp + a, s * n_grp + b) for s in range(n_shard) for a, b in pairs_of(s % 2)]

    partner = swap(lambda core: [(p, p ^ 8) for p in range(n_grp)])
    edges = swap(lambda core: [(p, (p + 1 - 2 * core) % n_grp) for p in range(n_grp)])
    fetch = [swap(lambda core: [(f[t], t) for t in range(n_grp)]) for f in FETCH]
    smem = pl.BlockSpec(memory_space=pltpu.SMEM)
    vmem = pl.BlockSpec(memory_space=pltpu.VMEM)

    def body(embeddings, cluster_ids, order):
        rows, width = embeddings.shape
        bf16, f32 = jnp.bfloat16, jnp.float32
        me = lax.axis_index("grp")
        core = lax.axis_index("shard") & 1
        table = jnp.array([[t] + [f[t] for f in FETCH] for t in range(n_grp)], jnp.int32)
        place = jnp.concatenate([jnp.stack([me, core]), table[me]]).astype(jnp.int32)
        msg, edge, meta = pl.pallas_call(
            pack_kernel,
            out_shape=(
                jax.ShapeDtypeStruct((HALF, width + META), bf16),
                jax.ShapeDtypeStruct((EDGE, width + META), bf16),
                jax.ShapeDtypeStruct((rows, META), bf16),
            ),
            in_specs=[smem, vmem, vmem, vmem],
            out_specs=(vmem, vmem, vmem),
            compiler_params=pltpu.CompilerParams(vmem_limit_bytes=32 << 20),
            name="pack",
        )(place, embeddings, cluster_ids.reshape(1, rows), order.reshape(1, rows))
        msg = lax.ppermute(msg, axes, partner)
        edge = lax.ppermute(edge, axes, edges)
        mine = pl.pallas_call(
            merge_kernel,
            grid_spec=pltpu.PrefetchScalarGridSpec(
                num_scalar_prefetch=1,
                grid=(1,),
                in_specs=[
                    pl.BlockSpec((HALF, width), lambda i, place: (place[0] // 8, 0)),
                    pl.BlockSpec((rows, META), lambda i, place: (0, 0)),
                    pl.BlockSpec((HALF, width + META), lambda i, place: (0, 0)),
                ],
                out_specs=pl.BlockSpec((HALF, width + META), lambda i, place: (0, 0)),
            ),
            out_shape=jax.ShapeDtypeStruct((HALF, width + META), bf16),
            compiler_params=pltpu.CompilerParams(vmem_limit_bytes=32 << 20),
            name="merge",
        )(place, embeddings, meta, msg)
        got = [lax.ppermute(mine, axes, f) for f in fetch]
        total = rows + EDGE + HALF
        near = pl.pallas_call(
            near_kernel,
            out_shape=jax.ShapeDtypeStruct((8, total), f32),
            in_specs=[vmem] * 4,
            out_specs=vmem,
            scratch_shapes=[pltpu.VMEM((total, width), bf16), pltpu.VMEM((total, META), bf16)],
            compiler_params=pltpu.CompilerParams(vmem_limit_bytes=32 << 20),
            cost_estimate=pl.CostEstimate(flops=2 * total * total * width, bytes_accessed=2 * total * width, transcendentals=0),
            name="near",
        )(embeddings, meta, edge, msg)
        blocks = [mine] + got
        chunk = min(1024, width)
        table = pl.pallas_call(
            far_kernel,
            grid_spec=pltpu.PrefetchScalarGridSpec(
                num_scalar_prefetch=1,
                grid=(width // chunk,),
                in_specs=[pl.BlockSpec((HALF, chunk), lambda i, place: (0, i))] * 5
                + [pl.BlockSpec((HALF, META), lambda i, place: (0, width // META))] * 5
                + [pl.BlockSpec((8, total), lambda i, place: (0, 0))],
                out_specs=pl.BlockSpec((16, rows), lambda i, place: (0, 0)),
                scratch_shapes=[pltpu.VMEM((5 * HALF, 5 * HALF), f32)],
            ),
            out_shape=jax.ShapeDtypeStruct((16, rows), f32),
            compiler_params=pltpu.CompilerParams(vmem_limit_bytes=32 << 20),
            name="far",
        )(place, *blocks, *blocks, near)
        table = lax.all_to_all(table, "grp", 0, 0, tiled=True)
        return jnp.max(table, axis=0)

    return jax.shard_map(
        body,
        mesh=mesh,
        in_specs=(P(axes, None), P(axes), P(axes)),
        out_specs=P(axes),
        check_vma=False,
    )
```

time: 162 us -> 89.1 us (0.55)
  the two profiles are of different devices: /device:TPU:1 before, /device:TPU:480 now
where the time goes in v1:
time: 89.1 us; the launch traced here: 88.7 us
  waiting for transfers between devices  37.7 us (42%)
  starting transfers between devices  20.7 us (23%)
  blocking collectives  18.6 us (21%)
  Pallas kernels  8.47 us (10%)
  local copies, waits for them, and re-layouts  2.59 us (3%)
    ppermute x4, waiting for transfers between devices, body(): got = [lax.ppermute(mine, axes, f) for f in fetch]  19.5 us
    all_to_all x1, blocking collectives, body(): table = lax.all_to_all(table, 'grp', 0, 0, tiled=True)  18.6 us
    ppermute x1, waiting for transfers between devices, body(): msg = lax.ppermute(msg, axes, partner)  18.2 us
    ppermute x4, starting transfers between devices, body(): got = [lax.ppermute(mine, axes, f) for f in fetch]  12.2 us
    ppermute x1, starting transfers between devices, body(): msg = lax.ppermute(msg, axes, partner)  5.1 us
    pallas_call x1, Pallas kernels, body(): pl.pallas_call(far_kernel, grid_spec=pltpu.PrefetchScalarGridSpec(num_sca...  4.35 us
    ppermute x1, starting transfers between devices, body(): edge = lax.ppermute(edge, axes, edges)  3.4 us
    pallas_call x1, Pallas kernels, body(): pl.pallas_call(near_kernel, out_shape=jax.ShapeDtypeStruct((8, total), f3...  2.24 us
  transfers between devices with their start and end apart: 6, of which 5 were waited for; matrix products, arithmetic and copies ran while one was open for 0% of the time, Pallas kernels for 4%

profile of v1, /device:TPU:480, one launch (start us, length us, event | category | flops | bytes accessed | tf_op | source)
XLA Modules:
  0.0 88.7 jit_solution(7833668174108373118)
XLA Ops:
  0.0 0.7 dynamic-slice_bitcast_fusion
  0.7 0.1 pad_add_fusion.place
  0.8 0.7 copy-done.2
  1.4 0.0 copy-done.3
  1.4 1.2 %copy-done = bf16[128,4096]{1,0:T(8,128)(2,1)S(1)} copy-done((bf16[128,4096]{1,0:T(8,128)(2,1)S(1)}, bf16[128,4096]{1,0:T(8,128)(2,1)}, u32[]{:S(2)}) %copy-start) | copy-done | bytes 1048600
  2.7 0.8 pack.1
  3.5 5.1 %collective-permute-start = (bf16[64,4224]{1,0:T(8,128)(2,1)S(1)}, bf16[64,4224]{1,0:T(8,128)(2,1)S(1)}, u32[]{:S(2)}, u32[]{:S(2)}) collective-permute-start(bf16[64,4224]{1,0:T(8,128)(2,1)S(1)} %get-tuple-element.9), channel_id=1, source_target_pairs={{0,8},{1,9},{2,10},{3,11},{4,12},{5,13},{6,14},{7,15},{8,0},{9,1},... | collective-permute-start | bytes 1622024 | tf_op jit(solution)/shard_map/ppermute | solution.py:194
  8.6 3.4 %collective-permute-start.5 = (bf16[96,4224]{1,0:T(8,128)(2,1)S(1)}, bf16[96,4224]{1,0:T(8,128)(2,1)S(1)}, u32[]{:S(2)}, u32[]{:S(2)}) collective-permute-start(bf16[96,4224]{1,0:T(8,128)(2,1)S(1)} %get-tuple-element.10), channel_id=1, source_target_pairs={{0,1},{1,2},{2,3},{3,4},{4,5},{5,6},{6,7},{7,8},{8,9},{9,10},{10,1... | collective-permute-start | bytes 2433032 | tf_op jit(solution)/shard_map/ppermute | solution.py:195
  12.0 18.2 %collective-permute-done.msg = bf16[64,4224]{1,0:T(8,128)(2,1)S(1)} collective-permute-done((bf16[64,4224]{1,0:T(8,128)(2,1)S(1)}, bf16[64,4224]{1,0:T(8,128)(2,1)S(1)}, u32[]{:S(2)}, u32[]{:S(2)}) %collective-permute-start) | collective-permute-done | bytes 540704 | tf_op jit(solution)/shard_map/ppermute | solution.py:194
  30.2 1.1 %merge.1.refs_0_.refs_5_ = bf16[64,4224]{1,0:T(8,128)(2,1)S(1)} custom-call(s32[7]{0:T(128)S(1)} %pad_add_fusion.place, bf16[128,4096]{1,0:T(8,128)(2,1)S(1)} %copy-done, bf16[128,128]{1,0:T(8,128)(2,1)S(1)} %get-tuple-element.8.own_meta, bf16[64,4224]{1,0:T(8,128)(2,1)S(1)} %collective-permute-done.msg), custom_call_target="tpu_custom_call" | custom-call | tf_op jit(solution)/shard_map/merge/pallas_call | solution.py:196
  31.3 1.9 %collective-permute-start.1 = (bf16[64,4224]{1,0:T(8,128)(2,1)S(1)}, bf16[64,4224]{1,0:T(8,128)(2,1)S(1)}, u32[]{:S(2)}, u32[]{:S(2)}) collective-permute-start(bf16[64,4224]{1,0:T(8,128)(2,1)S(1)} %merge.1.refs_0_.refs_5_), channel_id=1, source_target_pairs={{3,0},{8,1},{14,2},{15,3},{7,4},{1,5},{11,6},{4,7},{9,8},{5,9},{6,... | collective-permute-start | bytes 1622024 | tf_op jit(solution)/shard_map/ppermute | solution.py:212
  33.2 1.9 %collective-permute-start.2 = (bf16[64,4224]{1,0:T(8,128)(2,1)S(1)}, bf16[64,4224]{1,0:T(8,128)(2,1)S(1)}, u32[]{:S(2)}, u32[]{:S(2)}) collective-permute-start(bf16[64,4224]{1,0:T(8,128)(2,1)S(1)} %merge.1.refs_0_.refs_5_), channel_id=1, source_target_pairs={{12,0},{5,1},{3,2},{6,3},{1,4},{10,5},{2,6},{13,7},{7,8},{4,9},{14... | collective-permute-start | bytes 1622024 | tf_op jit(solution)/shard_map/ppermute | solution.py:212
  35.1 6.5 %collective-permute-start.3 = (bf16[64,4224]{1,0:T(8,128)(2,1)S(1)}, bf16[64,4224]{1,0:T(8,128)(2,1)S(1)}, u32[]{:S(2)}, u32[]{:S(2)}) collective-permute-start(bf16[64,4224]{1,0:T(8,128)(2,1)S(1)} %merge.1.refs_0_.refs_5_), channel_id=1, source_target_pairs={{5,0},{6,1},{1,2},{4,3},{0,4},{8,5},{7,6},{11,7},{12,8},{13,9},{9,... | collective-permute-start | bytes 1622024 | tf_op jit(solution)/shard_map/ppermute | solution.py:212
  41.6 1.9 %collective-permute-start.4 = (bf16[64,4224]{1,0:T(8,128)(2,1)S(1)}, bf16[64,4224]{1,0:T(8,128)(2,1)S(1)}, u32[]{:S(2)}, u32[]{:S(2)}) collective-permute-start(bf16[64,4224]{1,0:T(8,128)(2,1)S(1)} %merge.1.refs_0_.refs_5_), channel_id=1, source_target_pairs={{15,0},{13,1},{10,2},{2,3},{6,4},{4,5},{5,6},{3,7},{11,8},{14,9},{... | collective-permute-start | bytes 1622024 | tf_op jit(solution)/shard_map/ppermute | solution.py:212
  43.5 0.0 collective-permute-done.5.edge
  43.5 0.0 copy-done.1
  43.5 2.2 %near.1.refs_10_ = f32[8,288]{1,0:T(8,128)S(1)} custom-call(bf16[128,4096]{1,0:T(8,128)(2,1)S(1)} %copy-done.1, bf16[128,128]{1,0:T(8,128)(2,1)S(1)} %get-tuple-element.8.own_meta, bf16[96,4224]{1,0:T(8,128)(2,1)S(1)} %collective-permute-done.5.edge, bf16[64,4224]{1,0:T(8,128)(2,1)S(1)} %collective-permute-done.msg), custom_call_target="tpu_custom_call" | custom-call | flops 679477248 | bytes 2359296 | tf_op jit(solution)/shard_map/near/pallas_call | solution.py:214
  45.8 1.7 %collective-permute-done.1.refs_1_.refs_6_ = bf16[64,4224]{1,0:T(8,128)(2,1)S(1)} collective-permute-done((bf16[64,4224]{1,0:T(8,128)(2,1)S(1)}, bf16[64,4224]{1,0:T(8,128)(2,1)S(1)}, u32[]{:S(2)}, u32[]{:S(2)}) %collective-permute-start.1) | collective-permute-done | bytes 540704 | tf_op jit(solution)/shard_map/ppermute | solution.py:212
  47.5 1.9 %collective-permute-done.2.refs_2_.refs_7_ = bf16[64,4224]{1,0:T(8,128)(2,1)S(1)} collective-permute-done((bf16[64,4224]{1,0:T(8,128)(2,1)S(1)}, bf16[64,4224]{1,0:T(8,128)(2,1)S(1)}, u32[]{:S(2)}, u32[]{:S(2)}) %collective-permute-start.2) | collective-permute-done | bytes 540704 | tf_op jit(solution)/shard_map/ppermute | solution.py:212
  49.4 13.1 %collective-permute-done.3.refs_3_.refs_8_ = bf16[64,4224]{1,0:T(8,128)(2,1)S(1)} collective-permute-done((bf16[64,4224]{1,0:T(8,128)(2,1)S(1)}, bf16[64,4224]{1,0:T(8,128)(2,1)S(1)}, u32[]{:S(2)}, u32[]{:S(2)}) %collective-permute-start.3) | collective-permute-done | bytes 540704 | tf_op jit(solution)/shard_map/ppermute | solution.py:212
  62.4 2.8 %collective-permute-done.4.refs_4_.refs_9_ = bf16[64,4224]{1,0:T(8,128)(2,1)S(1)} collective-permute-done((bf16[64,4224]{1,0:T(8,128)(2,1)S(1)}, bf16[64,4224]{1,0:T(8,128)(2,1)S(1)}, u32[]{:S(2)}, u32[]{:S(2)}) %collective-permute-start.4) | collective-permute-done | bytes 540704 | tf_op jit(solution)/shard_map/ppermute | solution.py:212
  65.3 4.4 %far.1 = f32[16,128]{1,0:T(8,128)S(1)} custom-call(s32[7]{0:T(128)S(1)} %pad_add_fusion.place, bf16[64,4224]{1,0:T(8,128)(2,1)S(1)} %merge.1.refs_0_.refs_5_, bf16[64,4224]{1,0:T(8,128)(2,1)S(1)} %collective-permute-done.1.refs_1_.refs_6_, bf16[64,4224]{1,0:T(8,128)(2,1)S(1)} %collective-permute-done.2.refs_2_.refs_7_, ...), custom_call_target="tpu_custom_call" | custom-call | tf_op jit(solution)/shard_map/far/pallas_call | solution.py:226
  69.6 18.6 %all_to_all.9 = f32[16,1,128]{2,1,0:T(1,128)S(1)} all-to-all(f32[16,1,128]{2,1,0:T(1,128)S(1)} %bitcast.9), channel_id=1, replica_groups=mesh['shard'=32,'grp'=16] {'grp'}, dimensions={0} | all-to-all | bytes 16384 | tf_op jit(solution)/shard_map/all_to_all | solution.py:241
  88.2 0.5 reduce_max.9
  (4 shorter events, 0.0 us)
Async XLA Ops:
  0.8 0.7 copy-start.2
  0.8 0.7 copy-start.3
  1.4 1.2 %copy-start = (bf16[128,4096]{1,0:T(8,128)(2,1)S(1)}, bf16[128,4096]{1,0:T(8,128)(2,1)}, u32[]{:S(2)}) copy-start(bf16[128,4096]{1,0:T(8,128)(2,1)} %emb.3) | copy-start | bytes 3145732
  3.5 26.7 %collective-permute-start = (bf16[64,4224]{1,0:T(8,128)(2,1)S(1)}, bf16[64,4224]{1,0:T(8,128)(2,1)S(1)}, u32[]{:S(2)}, u32[]{:S(2)}) collective-permute-start(bf16[64,4224]{1,0:T(8,128)(2,1)S(1)} %get-tuple-element.9), channel_id=1, source_target_pairs={{0,8},{1,9},{2,10},{3,11},{4,12},{5,13},{6,14},{7,15},{8,0},{9,1},... | collective-permute-start | bytes 1622024 | tf_op jit(solution)/shard_map/ppermute | solution.py:194
  8.6 34.9 %collective-permute-start.5 = (bf16[96,4224]{1,0:T(8,128)(2,1)S(1)}, bf16[96,4224]{1,0:T(8,128)(2,1)S(1)}, u32[]{:S(2)}, u32[]{:S(2)}) collective-permute-start(bf16[96,4224]{1,0:T(8,128)(2,1)S(1)} %get-tuple-element.10), channel_id=1, source_target_pairs={{0,1},{1,2},{2,3},{3,4},{4,5},{5,6},{6,7},{7,8},{8,9},{9,10},{10,1... | collective-permute-start | bytes 2433032 | tf_op jit(solution)/shard_map/ppermute | solution.py:195
  30.2 13.3 %copy-start.1 = (bf16[128,4096]{1,0:T(8,128)(2,1)S(1)}, bf16[128,4096]{1,0:T(8,128)(2,1)}, u32[]{:S(2)}) copy-start(bf16[128,4096]{1,0:T(8,128)(2,1)} %emb.3) | copy-start | bytes 3145732
  31.3 16.2 %collective-permute-start.1 = (bf16[64,4224]{1,0:T(8,128)(2,1)S(1)}, bf16[64,4224]{1,0:T(8,128)(2,1)S(1)}, u32[]{:S(2)}, u32[]{:S(2)}) collective-permute-start(bf16[64,4224]{1,0:T(8,128)(2,1)S(1)} %merge.1.refs_0_.refs_5_), channel_id=1, source_target_pairs={{3,0},{8,1},{14,2},{15,3},{7,4},{1,5},{11,6},{4,7},{9,8},{5,9},{6,... | collective-permute-start | bytes 1622024 | tf_op jit(solution)/shard_map/ppermute | solution.py:212
  33.2 16.2 %collective-permute-start.2 = (bf16[64,4224]{1,0:T(8,128)(2,1)S(1)}, bf16[64,4224]{1,0:T(8,128)(2,1)S(1)}, u32[]{:S(2)}, u32[]{:S(2)}) collective-permute-start(bf16[64,4224]{1,0:T(8,128)(2,1)S(1)} %merge.1.refs_0_.refs_5_), channel_id=1, source_target_pairs={{12,0},{5,1},{3,2},{6,3},{1,4},{10,5},{2,6},{13,7},{7,8},{4,9},{14... | collective-permute-start | bytes 1622024 | tf_op jit(solution)/shard_map/ppermute | solution.py:212
  35.1 27.3 %collective-permute-start.3 = (bf16[64,4224]{1,0:T(8,128)(2,1)S(1)}, bf16[64,4224]{1,0:T(8,128)(2,1)S(1)}, u32[]{:S(2)}, u32[]{:S(2)}) collective-permute-start(bf16[64,4224]{1,0:T(8,128)(2,1)S(1)} %merge.1.refs_0_.refs_5_), channel_id=1, source_target_pairs={{5,0},{6,1},{1,2},{4,3},{0,4},{8,5},{7,6},{11,7},{12,8},{13,9},{9,... | collective-permute-start | bytes 1622024 | tf_op jit(solution)/shard_map/ppermute | solution.py:212
  41.6 23.7 %collective-permute-start.4 = (bf16[64,4224]{1,0:T(8,128)(2,1)S(1)}, bf16[64,4224]{1,0:T(8,128)(2,1)S(1)}, u32[]{:S(2)}, u32[]{:S(2)}) collective-permute-start(bf16[64,4224]{1,0:T(8,128)(2,1)S(1)} %merge.1.refs_0_.refs_5_), channel_id=1, source_target_pairs={{15,0},{13,1},{10,2},{2,3},{6,4},{4,5},{5,6},{3,7},{11,8},{14,9},{... | collective-permute-start | bytes 1622024 | tf_op jit(solution)/shard_map/ppermute | solution.py:212

commit v2 on v0

v2 whole, which is shorter than its diff:
```python
import functools

import jax
import jax.numpy as jnp
from jax import lax
from jax.experimental import pallas as pl
from jax.experimental.pallas import tpu as pltpu
from jax.sharding import PartitionSpec as P

META = 128

FETCH = (
    (
        (0, 5, 1, 2, 6, 4, 10, 3, 9, 12, 14, 7, 13, 8, 15, 11),
        (0, 13, 3, 7, 8, 1, 2, 5, 4, 9, 11, 10, 12, 14, 6, 15),
        (8, 0, 1, 4, 12, 7, 5, 6, 11, 10, 3, 15, 14, 2, 9, 13),
        (1, 6, 15, 0, 5, 9, 4, 11, 3, 13, 10, 8, 7, 14, 2, 12),
    ),
    (
        (1, 2, 8, 12, 7, 11, 4, 3, 13, 5, 6, 10, 14, 9, 15, 0),
        (12, 5, 2, 7, 4, 6, 9, 8, 11, 10, 14, 15, 0, 1, 13, 3),
        (3, 1, 0, 10, 5, 12, 2, 6, 4, 8, 13, 9, 15, 14, 7, 11),
        (4, 13, 6, 2, 0, 5, 10, 1, 9, 3, 11, 7, 8, 12, 14, 15),
    ),
)
COUNT = len(FETCH[0])


def dot_nt(left, right):
    return lax.dot_general(left, right, (((1,), (1,)), ((), ())), preferred_element_type=jnp.float32)


def pair_form(first):
    a = lax.broadcasted_iota(jnp.int32, (META, META), 0)
    b = lax.broadcasted_iota(jnp.int32, (META, META), 1)
    plus = ((a == first) & (b == 2)) | ((a == first + 1) & (b == 3))
    minus = ((a == 2) & (b == first)) | ((a == 3) & (b == first + 1))
    return jnp.where(plus, 1.0, jnp.where(minus, -1.0, 0.0)).astype(jnp.bfloat16)


def difference(left, right, first):
    turned = jnp.dot(left, pair_form(first), preferred_element_type=jnp.float32)
    return dot_nt(turned.astype(jnp.bfloat16), right)


def pack_kernel(emb, ids, order, msg):
    rows, width = emb.shape
    row = lax.broadcasted_iota(jnp.int32, (8, rows), 0)
    value = jnp.where(row < 2, jnp.broadcast_to(order[...], (8, rows)), jnp.broadcast_to(ids[...], (8, rows)))
    low = value & 127
    parts = jnp.where((row & 1) == 0, value - low, low)
    parts = jnp.where((row == 2) | (row == 3), 1, parts)
    parts = jnp.where(row < 6, parts, 0).astype(jnp.float32)
    wide = jnp.concatenate([parts, jnp.zeros((META - 8, rows), jnp.float32)], axis=0)
    msg[:, width:] = wide.T.astype(jnp.bfloat16)
    for at in range(0, rows, 32):
        block = emb[at : at + 32, :].astype(jnp.float32)
        squares = jnp.sum(block * block, axis=1, keepdims=True)
        msg[at : at + 32, :width] = (block * lax.rsqrt(squares + 1e-06)).astype(jnp.bfloat16)


def meet(olds, new, scores):
    rows = new.shape[0]
    width = new.shape[1] - META
    blocks = [*olds, new]
    chunk = min(1024, width)
    for at in range(0, width, chunk):
        part = jnp.concatenate([b[:, at : at + chunk] for b in blocks], axis=0)
        product = dot_nt(new[:, at : at + chunk], part)
        if at == 0:
            scores[...] = product
        else:
            scores[...] += product
    meta = jnp.concatenate([b[:, width:] for b in blocks], axis=0)
    mine = new[:, width:]
    ahead = difference(mine, meta, 0)
    same = difference(mine, meta, 4) == 0
    value = scores[...]
    down = jnp.max(jnp.where(same & (ahead < 0), value, -1.0), axis=0, keepdims=True)
    across = jnp.where(same & (ahead > 0), value, -1.0)
    most = functools.reduce(jnp.maximum, [across[:, k * rows : (k + 1) * rows] for k in range(len(blocks))])
    turned = jnp.max(most.T, axis=0, keepdims=True)
    return down, turned


def meet_kernel(count, *refs):
    olds, new, before, out, scores = refs[:count], refs[count], refs[count + 1 : -2], refs[-2], refs[-1]
    rows = new.shape[0]
    down, turned = meet(olds, new, scores)
    if before:
        down = jnp.maximum(down, jnp.concatenate([before[0][0:1], turned], axis=1))
    else:
        down = jnp.maximum(down, turned)
    out[...] = jnp.broadcast_to(down, out.shape)


def last_kernel(count, table, *refs):
    olds, new, before, out, scores = refs[:count], refs[count], refs[count + 1], refs[-2], refs[-1]
    rows = new.shape[0]
    down, turned = meet(olds, new, scores)
    down = jnp.maximum(down, jnp.concatenate([before[0:1], turned], axis=1))
    me = lax.axis_index("grp")
    place = (lax.axis_index("shard") & 1) * 16 + me
    dest = lax.broadcasted_iota(jnp.int32, (16, rows), 0)
    total = jnp.where(dest == me, down[:, :rows], -1.0)
    for k in range(count):
        piece = down[:, (k + 1) * rows : (k + 2) * rows]
        total = jnp.maximum(total, jnp.where(dest == table[place, k], piece, -1.0))
    out[...] = total


def solution(mesh):
    n_shard, n_grp = mesh.shape["shard"], mesh.shape["grp"]
    axes = ("shard", "grp")

    def pairs(k):
        return [
            (s * n_grp + FETCH[s % 2][k][t], s * n_grp + t)
            for s in range(n_shard)
            for t in range(n_grp)
            if FETCH[s % 2][k][t] != t
        ]

    smem = pl.BlockSpec(memory_space=pltpu.SMEM)
    vmem = pl.BlockSpec(memory_space=pltpu.VMEM)
    params = pltpu.CompilerParams(vmem_limit_bytes=32 << 20)

    def body(embeddings, cluster_ids, order):
        rows, width = embeddings.shape
        f32 = jnp.float32
        mine = pl.pallas_call(
            pack_kernel,
            out_shape=jax.ShapeDtypeStruct((rows, width + META), jnp.bfloat16),
            in_specs=[vmem] * 3,
            out_specs=vmem,
            compiler_params=params,
            name="pack",
        )(embeddings, cluster_ids.reshape(1, rows), order.reshape(1, rows))
        blocks = [mine] + [lax.ppermute(mine, axes, pairs(k)) for k in range(COUNT)]
        table = jnp.array([[f[k][t] for k in range(COUNT)] for f in FETCH for t in range(n_grp)], jnp.int32)
        best = []
        for count in range(COUNT + 1):
            total = (count + 1) * rows
            last = count == COUNT
            kernel = functools.partial(last_kernel if last else meet_kernel, count)
            out = (n_grp, rows) if last else (8, total)
            best = [
                pl.pallas_call(
                    kernel,
                    out_shape=jax.ShapeDtypeStruct(out, f32),
                    in_specs=[smem] * last + [vmem] * (count + 1 + len(best)),
                    out_specs=vmem,
                    scratch_shapes=[pltpu.VMEM((rows, total), f32)],
                    compiler_params=params,
                    cost_estimate=pl.CostEstimate(flops=2 * rows * total * width, bytes_accessed=2 * total * width, transcendentals=0),
                    name="meet_%d" % count,
                )(*([table] if last else []), *blocks[: count + 1], *best)
            ]
        given = lax.all_to_all(best[0], "grp", 0, 0, tiled=True)
        return jnp.max(given, axis=0)

    return jax.shard_map(
        body,
        mesh=mesh,
        in_specs=(P(axes, None), P(axes), P(axes)),
        out_specs=P(axes),
        check_vma=False,
    )
```

time: 162 us -> 66 us (0.41)
  the two profiles are of different devices: /device:TPU:1 before, /device:TPU:256 now
where the time goes in v2:
time: 66 us; the launch traced here: 65.8 us
  waiting for transfers between devices  20.3 us (31%)
  blocking collectives  17.6 us (27%)
  starting transfers between devices  16.3 us (25%)
  Pallas kernels  8.31 us (13%)
  local copies, waits for them, and re-layouts  2.54 us (4%)
    ppermute x4, waiting for transfers between devices, body(): blocks = [mine] + [lax.ppermute(mine, axes, pairs(k)) for k in range(COUNT)]  20.3 us
    all_to_all x1, blocking collectives, body(): given = lax.all_to_all(best[0], 'grp', 0, 0, tiled=True)  17.6 us
    ppermute x4, starting transfers between devices, body(): blocks = [mine] + [lax.ppermute(mine, axes, pairs(k)) for k in range(COUNT)]  16.3 us
    pallas_call x5, Pallas kernels, body(): pl.pallas_call(kernel, out_shape=jax.ShapeDtypeStruct(out, f32), in_specs...  7.96 us
    unnamed x8, local copies, waits for them, and re-layouts  2.54 us
  transfers between devices with their start and end apart: 4, of which 2 were waited for; matrix products, arithmetic and copies ran while one was open for 0% of the time, Pallas kernels for 8%

profile of v2, /device:TPU:256, one launch (start us, length us, event | category | flops | bytes accessed | tf_op | source)
XLA Modules:
  0.0 65.8 jit_solution(4642767731845251744)
XLA Ops:
  0.0 0.0 copy-start
  0.0 1.2 %copy-done = bf16[128,4096]{1,0:T(8,128)(2,1)S(1)} copy-done((bf16[128,4096]{1,0:T(8,128)(2,1)S(1)}, bf16[128,4096]{1,0:T(8,128)(2,1)}, u32[]{:S(2)}) %copy-start) | copy-done | bytes 1048600
  1.2 0.0 copy-start.2
  1.2 0.7 copy-done.2
  1.9 0.0 copy-start.3
  1.9 0.7 copy-done.3
  2.5 0.4 pack.1.refs_0_
  2.9 0.7 %collective-permute-start = (bf16[128,4224]{1,0:T(8,128)(2,1)S(1)}, bf16[128,4224]{1,0:T(8,128)(2,1)S(1)}, u32[]{:S(2)}, u32[]{:S(2)}) collective-permute-start(bf16[128,4224]{1,0:T(8,128)(2,1)S(1)} %pack.1.refs_0_), channel_id=1, source_target_pairs={{5,1},{1,2},{2,3},{6,4},{4,5},{10,6},{3,7},{9,8},{12,9},{14,10},{7... | collective-permute-start | bytes 3244040 | tf_op jit(solution)/shard_map/ppermute | solution.py:139
  3.6 0.7 %collective-permute-start.1 = (bf16[128,4224]{1,0:T(8,128)(2,1)S(1)}, bf16[128,4224]{1,0:T(8,128)(2,1)S(1)}, u32[]{:S(2)}, u32[]{:S(2)}) collective-permute-start(bf16[128,4224]{1,0:T(8,128)(2,1)S(1)} %pack.1.refs_0_), channel_id=1, source_target_pairs={{13,1},{3,2},{7,3},{8,4},{1,5},{2,6},{5,7},{4,8},{11,10},{10,11},{... | collective-permute-start | bytes 3244040 | tf_op jit(solution)/shard_map/ppermute | solution.py:139
  4.4 7.8 %collective-permute-start.2 = (bf16[128,4224]{1,0:T(8,128)(2,1)S(1)}, bf16[128,4224]{1,0:T(8,128)(2,1)S(1)}, u32[]{:S(2)}, u32[]{:S(2)}) collective-permute-start(bf16[128,4224]{1,0:T(8,128)(2,1)S(1)} %pack.1.refs_0_), channel_id=1, source_target_pairs={{8,0},{0,1},{1,2},{4,3},{12,4},{7,5},{5,6},{6,7},{11,8},{10,9},{3,... | collective-permute-start | bytes 3244040 | tf_op jit(solution)/shard_map/ppermute | solution.py:139
  12.2 7.1 %collective-permute-start.3 = (bf16[128,4224]{1,0:T(8,128)(2,1)S(1)}, bf16[128,4224]{1,0:T(8,128)(2,1)S(1)}, u32[]{:S(2)}, u32[]{:S(2)}) collective-permute-start(bf16[128,4224]{1,0:T(8,128)(2,1)S(1)} %pack.1.refs_0_), channel_id=1, source_target_pairs={{1,0},{6,1},{15,2},{0,3},{5,4},{9,5},{4,6},{11,7},{3,8},{13,9},{8,... | collective-permute-start | bytes 3244040 | tf_op jit(solution)/shard_map/ppermute | solution.py:139
  19.3 0.7 %meet_0.1.refs_2_ = f32[8,128]{1,0:T(8,128)S(1)} custom-call(bf16[128,4224]{1,0:T(8,128)(2,1)S(1)} %pack.1.refs_0_), custom_call_target="tpu_custom_call" | custom-call | flops 134217728 | bytes 1048576 | tf_op jit(solution)/shard_map/meet_0/pallas_call | solution.py:148
  20.0 0.0 collective-permute-done.refs_1_
  20.0 1.1 %meet_1.1.refs_3_ = f32[8,256]{1,0:T(8,128)S(1)} custom-call(bf16[128,4224]{1,0:T(8,128)(2,1)S(1)} %pack.1.refs_0_, bf16[128,4224]{1,0:T(8,128)(2,1)S(1)} %collective-permute-done.refs_1_, f32[8,128]{1,0:T(8,128)S(1)} %meet_0.1.refs_2_), custom_call_target="tpu_custom_call" | custom-call | flops 268435456 | bytes 2097152 | tf_op jit(solution)/shard_map/meet_1/pallas_call | solution.py:148
  21.1 0.0 collective-permute-done.1.refs_2_
  21.1 1.4 %meet_2.1.refs_4_ = f32[8,384]{1,0:T(8,128)S(1)} custom-call(bf16[128,4224]{1,0:T(8,128)(2,1)S(1)} %pack.1.refs_0_, bf16[128,4224]{1,0:T(8,128)(2,1)S(1)} %collective-permute-done.refs_1_, bf16[128,4224]{1,0:T(8,128)(2,1)S(1)} %collective-permute-done.1.refs_2_, f32[8,256]{1,0:T(8,128)S(1)} %meet_1.1.refs_3_), custom_call_target="tpu_custom_call" | custom-call | flops 402653184 | bytes 3145728 | tf_op jit(solution)/shard_map/meet_2/pallas_call | solution.py:148
  22.5 0.0 copy-start.1
  22.5 13.3 %collective-permute-done.2.refs_3_ = bf16[128,4224]{1,0:T(8,128)(2,1)S(1)} collective-permute-done((bf16[128,4224]{1,0:T(8,128)(2,1)S(1)}, bf16[128,4224]{1,0:T(8,128)(2,1)S(1)}, u32[]{:S(2)}, u32[]{:S(2)}) %collective-permute-start.2) | collective-permute-done | bytes 1081376 | tf_op jit(solution)/shard_map/ppermute | solution.py:139
  35.9 1.9 %meet_3.1.refs_5_ = f32[8,512]{1,0:T(8,128)S(1)} custom-call(bf16[128,4224]{1,0:T(8,128)(2,1)S(1)} %pack.1.refs_0_, bf16[128,4224]{1,0:T(8,128)(2,1)S(1)} %collective-permute-done.refs_1_, bf16[128,4224]{1,0:T(8,128)(2,1)S(1)} %collective-permute-done.1.refs_2_, bf16[128,4224]{1,0:T(8,128)(2,1)S(1)} %collective-permute-done.2.refs_3_, ...), custom_call_target="tpu_custom_call" | custom-call | flops 536870912 | bytes 4194304 | tf_op jit(solution)/shard_map/meet_3/pallas_call | solution.py:148
  37.8 7.0 %collective-permute-done.3.refs_4_ = bf16[128,4224]{1,0:T(8,128)(2,1)S(1)} collective-permute-done((bf16[128,4224]{1,0:T(8,128)(2,1)S(1)}, bf16[128,4224]{1,0:T(8,128)(2,1)S(1)}, u32[]{:S(2)}, u32[]{:S(2)}) %collective-permute-start.3) | collective-permute-done | bytes 1081376 | tf_op jit(solution)/shard_map/ppermute | solution.py:139
  44.7 0.0 copy-done.1
  44.7 2.9 %meet_4.1 = f32[16,128]{1,0:T(8,128)S(1)} custom-call(s32[32,4]{1,0:T(8,128)S(1)} %copy-done.1, bf16[128,4224]{1,0:T(8,128)(2,1)S(1)} %pack.1.refs_0_, bf16[128,4224]{1,0:T(8,128)(2,1)S(1)} %collective-permute-done.refs_1_, bf16[128,4224]{1,0:T(8,128)(2,1)S(1)} %collective-permute-done.1.refs_2_, bf16[128,4224]{1,0:T(8,128)(2,1)S(1)} %collective-permute-done.2.refs_3_, ...), custom_call_target="tpu_custom_call" | custom-call | flops 671088640 | bytes 5242880 | tf_op jit(solution)/shard_map/meet_4/pallas_call | solution.py:148
  47.6 17.6 %all_to_all.9 = f32[16,1,128]{2,1,0:T(1,128)S(1)} all-to-all(f32[16,1,128]{2,1,0:T(1,128)S(1)} %bitcast.5), channel_id=1, replica_groups=mesh['shard'=32,'grp'=16] {'grp'}, dimensions={0} | all-to-all | bytes 16384 | tf_op jit(solution)/shard_map/all_to_all | solution.py:159
  65.2 0.5 reduce_max.9
Async XLA Ops:
  0.0 1.2 %copy-start = (bf16[128,4096]{1,0:T(8,128)(2,1)S(1)}, bf16[128,4096]{1,0:T(8,128)(2,1)}, u32[]{:S(2)}) copy-start(bf16[128,4096]{1,0:T(8,128)(2,1)} %emb.1) | copy-start | bytes 3145732
  1.2 0.7 copy-start.2
  1.9 0.7 copy-start.3
  2.9 17.1 %collective-permute-start = (bf16[128,4224]{1,0:T(8,128)(2,1)S(1)}, bf16[128,4224]{1,0:T(8,128)(2,1)S(1)}, u32[]{:S(2)}, u32[]{:S(2)}) collective-permute-start(bf16[128,4224]{1,0:T(8,128)(2,1)S(1)} %pack.1.refs_0_), channel_id=1, source_target_pairs={{5,1},{1,2},{2,3},{6,4},{4,5},{10,6},{3,7},{9,8},{12,9},{14,10},{7... | collective-permute-start | bytes 3244040 | tf_op jit(solution)/shard_map/ppermute | solution.py:139
  3.6 17.5 %collective-permute-start.1 = (bf16[128,4224]{1,0:T(8,128)(2,1)S(1)}, bf16[128,4224]{1,0:T(8,128)(2,1)S(1)}, u32[]{:S(2)}, u32[]{:S(2)}) collective-permute-start(bf16[128,4224]{1,0:T(8,128)(2,1)S(1)} %pack.1.refs_0_), channel_id=1, source_target_pairs={{13,1},{3,2},{7,3},{8,4},{1,5},{2,6},{5,7},{4,8},{11,10},{10,11},{... | collective-permute-start | bytes 3244040 | tf_op jit(solution)/shard_map/ppermute | solution.py:139
  4.4 31.5 %collective-permute-start.2 = (bf16[128,4224]{1,0:T(8,128)(2,1)S(1)}, bf16[128,4224]{1,0:T(8,128)(2,1)S(1)}, u32[]{:S(2)}, u32[]{:S(2)}) collective-permute-start(bf16[128,4224]{1,0:T(8,128)(2,1)S(1)} %pack.1.refs_0_), channel_id=1, source_target_pairs={{8,0},{0,1},{1,2},{4,3},{12,4},{7,5},{5,6},{6,7},{11,8},{10,9},{3,... | collective-permute-start | bytes 3244040 | tf_op jit(solution)/shard_map/ppermute | solution.py:139
  12.2 32.6 %collective-permute-start.3 = (bf16[128,4224]{1,0:T(8,128)(2,1)S(1)}, bf16[128,4224]{1,0:T(8,128)(2,1)S(1)}, u32[]{:S(2)}, u32[]{:S(2)}) collective-permute-start(bf16[128,4224]{1,0:T(8,128)(2,1)S(1)} %pack.1.refs_0_), channel_id=1, source_target_pairs={{1,0},{6,1},{15,2},{0,3},{5,4},{9,5},{4,6},{11,7},{3,8},{13,9},{8,... | collective-permute-start | bytes 3244040 | tf_op jit(solution)/shard_map/ppermute | solution.py:139
  22.5 22.2 %copy-start.1 = (s32[32,4]{1,0:T(8,128)S(1)}, s32[32,4]{1,0:T(8,128)}, u32[]{:S(2)}) copy-start(s32[32,4]{1,0:T(8,128)} %constant.4.clone.table) | copy-start | bytes 1540

commit v3 on v0

v3 whole, which is shorter than its diff:
```python
import functools

import jax
import jax.numpy as jnp
from jax import lax
from jax.experimental import pallas as pl
from jax.experimental.pallas import tpu as pltpu
from jax.sharding import PartitionSpec as P

META = 128

ROUTE = (
    (
        (4, 2, 1, 0, 7, 6, 5, 3, 12, 10, 11, 8, 15, 9, 13, 14),
        (12, 5, 14, 15, 0, 4, 7, 11, 9, 8, 6, 10, 13, 1, 2, 3),
        (1, 0, 3, 2, 8, 4, 7, 11, 12, 5, 6, 15, 13, 9, 10, 14),
        (12, 5, 6, 0, 7, 9, 2, 3, 4, 10, 14, 8, 15, 1, 13, 11),
        (2, 0, 0, 0, 2, 2, 1, 1, 2, 2, 0, 2, 2, 1, 2, 1),
        (1, 2, 2, 2, 1, 1, 2, 2, 1, 2, 2, 1, 0, 1, 1, 2),
    ),
    (
        (1, 0, 3, 2, 5, 9, 10, 6, 4, 13, 14, 7, 8, 12, 15, 11),
        (3, 13, 6, 7, 8, 1, 2, 4, 11, 5, 9, 15, 0, 14, 10, 12),
        (3, 2, 1, 7, 0, 6, 5, 4, 9, 13, 11, 10, 8, 14, 15, 12),
        (4, 13, 14, 15, 5, 1, 10, 6, 11, 8, 9, 7, 0, 12, 2, 3),
        (2, 0, 2, 2, 2, 0, 2, 2, 1, 1, 2, 1, 1, 1, 2, 1),
        (1, 1, 1, 1, 1, 1, 1, 1, 2, 1, 1, 2, 1, 1, 2, 2),
    ),
)


def dot_nt(left, right):
    return lax.dot_general(left, right, (((1,), (1,)), ((), ())), preferred_element_type=jnp.float32)


def key_difference(left, right):
    a = lax.broadcasted_iota(jnp.int32, (META, META), 0)
    b = lax.broadcasted_iota(jnp.int32, (META, META), 1)
    plus = (b == a + 2) & ((a & 2) == 0)
    minus = (a == b + 2) & ((b & 2) == 0)
    size = jnp.where(a < 4, 1.0, jnp.where(a < 8, 4096.0, 0.0))
    form = jnp.where(plus, size, jnp.where(minus, -size, 0.0)).astype(jnp.bfloat16)
    turned = jnp.dot(left, form, preferred_element_type=jnp.float32)
    return dot_nt(turned.astype(jnp.bfloat16), right)


def pack_kernel(emb, numbers, *outs):
    rows, width = emb.shape
    row = lax.broadcasted_iota(jnp.int32, (16, rows), 0)
    value = jnp.where(row < 4, jnp.broadcast_to(numbers[1:2], (16, rows)), jnp.broadcast_to(numbers[0:1], (16, rows)))
    low = value & 127
    parts = jnp.where((row & 2) == 2, 1, jnp.where((row & 1) == 0, value - low, low))
    parts = jnp.where(row < 8, parts, lax.axis_index("grp")).astype(jnp.float32)
    wide = jnp.concatenate([parts, jnp.zeros((META - 16, rows), jnp.float32)], axis=0)
    meta = wide.T.astype(jnp.bfloat16)
    half = rows // 2
    for i, out in enumerate(outs):
        out[:, width:] = meta[i * half : (i + 1) * half]
        for at in range(0, half, 32):
            block = emb[i * half + at : i * half + at + 32, :].astype(jnp.float32)
            squares = jnp.sum(block * block, axis=1, keepdims=True)
            out[at : at + 32, :width] = (block * lax.rsqrt(squares + 1e-06)).astype(jnp.bfloat16)


def meet(blocks, count):
    width = blocks[0].shape[1] - META
    every = jnp.concatenate([b[:, :width] for b in blocks], axis=0)
    every_meta = jnp.concatenate([b[:, width:] for b in blocks], axis=0)
    new = jnp.concatenate([b[:, :width] for b in blocks[-count:]], axis=0)
    new_meta = jnp.concatenate([b[:, width:] for b in blocks[-count:]], axis=0)
    ahead = key_difference(new_meta, every_meta)
    scores = dot_nt(new, every)
    down = jnp.max(jnp.where((ahead < 0) & (ahead > -2048), scores, -1.0), axis=0, keepdims=True)
    if count == len(blocks):
        return down
    across = jnp.where((ahead > 0) & (ahead < 2048), scores, -1.0)
    lanes = new.shape[0]
    most = functools.reduce(jnp.maximum, [across[:, at : at + lanes] for at in range(0, across.shape[1], lanes)])
    turned = jnp.max(most.T, axis=0, keepdims=True)
    rest = jnp.full((1, down.shape[1] - lanes), -1.0, jnp.float32)
    return jnp.maximum(down, jnp.concatenate([rest, turned], axis=1))


def meet_kernel(number, count, *refs):
    blocks, before, out = refs[:number], refs[number:-1], refs[-1]
    best = meet(blocks, count)
    if before:
        old = before[0].shape[1]
        best = jnp.concatenate([jnp.maximum(best[:, :old], before[0][0:1]), best[:, old:]], axis=1)
    out[...] = jnp.broadcast_to(best, out.shape)


def last_kernel(number, count, *refs):
    blocks, before, out = refs[:number], refs[number], refs[-1]
    half, width = blocks[0].shape[0], blocks[0].shape[1] - META
    best = meet(blocks, count)
    old = before.shape[1]
    best = jnp.concatenate([jnp.maximum(best[:, :old], before[0:1]), best[:, old:]], axis=1)
    parts = [best[:, k * half : (k + 1) * half] for k in range(number)]
    dest = lax.broadcasted_iota(jnp.int32, (16, 2 * half), 0).astype(jnp.float32)
    total = jnp.full((16, 2 * half), -1.0, jnp.float32)
    for low, high in ((0, 1), (2, 3), (4, 5), (6, 8), (7, 9)):
        device = blocks[low][0:16, width:].astype(jnp.float32)[0:1, 8:9]
        value = jnp.concatenate([parts[low], parts[high]], axis=1)
        total = jnp.maximum(total, jnp.where(dest == device, value, -1.0))
    out[...] = total


def my_place():
    return (lax.axis_index("shard") & 1) * 16 + lax.axis_index("grp")


def signed(bits):
    return bits - (1 << 32) if bits >> 31 else bits


def choose_kernel(own, first, second, *outs):
    place = my_place()
    for j, out in enumerate(outs):
        for k, ref in enumerate((own, first, second)):
            users = sum(1 << (16 * c + t) for c in range(2) for t in range(16) if ROUTE[c][4 + j][t] == k)

            @pl.when(((jnp.int32(signed(users)) >> place) & 1) == 1)
            def _(ref=ref, out=out):
                out[...] = ref[...]


def solution(mesh):
    n_shard, n_grp = mesh.shape["shard"], mesh.shape["grp"]
    axes = ("shard", "grp")

    def pairs(k):
        return [(s * n_grp + ROUTE[s % 2][k][t], s * n_grp + t) for s in range(n_shard) for t in range(n_grp)]

    vmem = pl.BlockSpec(memory_space=pltpu.VMEM)
    params = pltpu.CompilerParams(vmem_limit_bytes=32 << 20)

    def body(embeddings, cluster_ids, order):
        rows, width = embeddings.shape
        half = rows // 2
        f32 = jnp.float32
        piece = jax.ShapeDtypeStruct((half, width + META), jnp.bfloat16)

        def meet_call(kernel, count, out, blocks, *before):
            flops = 2 * len(blocks) * count * half * half * width
            return pl.pallas_call(
                functools.partial(kernel, len(blocks), count),
                out_shape=jax.ShapeDtypeStruct(out, f32),
                in_specs=[vmem] * (len(blocks) + len(before)),
                out_specs=vmem,
                compiler_params=params,
                cost_estimate=pl.CostEstimate(flops=flops, bytes_accessed=2 * len(blocks) * half * width, transcendentals=0),
                name=kernel.__name__,
            )(*blocks, *before)

        own = pl.pallas_call(
            pack_kernel,
            out_shape=(piece, piece),
            in_specs=[vmem] * 2,
            out_specs=(vmem, vmem),
            compiler_params=params,
            name="pack",
        )(embeddings, jnp.stack([cluster_ids, order]))
        got = [[lax.ppermute(own[i], axes, pairs(k)) for k in (0, 1)] for i in (0, 1)]
        came = []
        for i in (0, 1):
            passed = pl.pallas_call(
                choose_kernel,
                out_shape=(piece, piece),
                in_specs=[vmem] * 3,
                out_specs=(vmem, vmem),
                compiler_params=params,
                name="choose",
            )(own[i], *got[i])
            came.append([lax.ppermute(passed[k], axes, pairs(2 + k)) for k in (0, 1)])
        near = [own[0], own[1], got[0][0], got[1][0], got[0][1], got[1][1]]
        best = meet_call(meet_kernel, 6, (8, 6 * half), near)
        best = meet_call(meet_kernel, 2, (8, 8 * half), near + came[0], best)
        table = meet_call(last_kernel, 2, (n_grp, rows), near + came[0] + came[1], best)
        given = lax.all_to_all(table, "grp", 0, 0, tiled=True)
        return jnp.max(given, axis=0)

    return jax.shard_map(
        body,
        mesh=mesh,
        in_specs=(P(axes, None), P(axes), P(axes)),
        out_specs=P(axes),
        check_vma=False,
    )
```

time: 162 us -> 61.7 us (0.38)
  the two profiles are of different devices: /device:TPU:1 before, /device:TPU:2 now
where the time goes in v3:
time: 61.7 us; the launch traced here: 61.3 us
  starting transfers between devices  32.6 us (53%)
  blocking collectives  12.5 us (20%)
  waiting for transfers between devices  7.41 us (12%)
  Pallas kernels  6.16 us (10%)
  local copies, waits for them, and re-layouts  1.89 us (3%)
    ppermute x4, starting transfers between devices, body(): came.append([lax.ppermute(passed[k], axes, pairs(2 + k)) for k in (0, 1)])  19.3 us
    ppermute x4, starting transfers between devices, body(): lax.ppermute(own[i], axes, pairs(k))  13.3 us
    all_to_all x1, blocking collectives, body(): given = lax.all_to_all(table, 'grp', 0, 0, tiled=True)  12.5 us
    ppermute x4, waiting for transfers between devices, body(): came.append([lax.ppermute(passed[k], axes, pairs(2 + k)) for k in (0, 1)])  5.61 us
    pallas_call x3, Pallas kernels, meet_call(): pl.pallas_call(functools.partial(kernel, len(blocks), count), out_shape=j...  5.6 us
    unnamed x6, local copies, waits for them, and re-layouts  1.89 us
    ppermute x4, waiting for transfers between devices, body(): lax.ppermute(own[i], axes, pairs(k))  1.81 us
  transfers between devices with their start and end apart: 8, of which 3 were waited for; matrix products, arithmetic and copies ran while one was open for 0% of the time, Pallas kernels for 6%

profile of v3, /device:TPU:2, one launch (start us, length us, event | category | flops | bytes accessed | tf_op | source)
XLA Modules:
  0.0 61.3 jit_solution(6524976811893981440)
XLA Ops:
  0.0 0.7 %copy-done.1 = s32[128]{0:T(128)S(1)} copy-done((s32[128]{0:T(128)S(1)}, s32[128]{0:T(128)}, u32[]{:S(2)}) %copy-start.1) | copy-done | bytes 536
  0.7 0.0 copy-done.2
  0.7 1.2 %copy-done = bf16[128,4096]{1,0:T(8,128)(2,1)S(1)} copy-done((bf16[128,4096]{1,0:T(8,128)(2,1)S(1)}, bf16[128,4096]{1,0:T(8,128)(2,1)}, u32[]{:S(2)}) %copy-start) | copy-done | bytes 1048600
  1.9 0.4 pack.1
  2.3 3.4 %collective-permute-start = (bf16[64,4224]{1,0:T(8,128)(2,1)S(1)}, bf16[64,4224]{1,0:T(8,128)(2,1)S(1)}, u32[]{:S(2)}, u32[]{:S(2)}) collective-permute-start(bf16[64,4224]{1,0:T(8,128)(2,1)S(1)} %get-tuple-element.11.own.refs_0_), channel_id=1, source_target_pairs={{4,0},{2,1},{1,2},{0,3},{7,4},{6,5},{5,6},{3,7},{12,8},{10,9},{11,... | collective-permute-start | bytes 1622024 | tf_op jit(solution)/shard_map/ppermute | solution.py:164
  5.7 4.9 %collective-permute-start.2 = (bf16[64,4224]{1,0:T(8,128)(2,1)S(1)}, bf16[64,4224]{1,0:T(8,128)(2,1)S(1)}, u32[]{:S(2)}, u32[]{:S(2)}) collective-permute-start(bf16[64,4224]{1,0:T(8,128)(2,1)S(1)} %get-tuple-element.11.own.refs_0_), channel_id=1, source_target_pairs={{12,0},{5,1},{14,2},{15,3},{0,4},{4,5},{7,6},{11,7},{9,8},{8,9},{6... | collective-permute-start | bytes 1622024 | tf_op jit(solution)/shard_map/ppermute | solution.py:164
  10.6 3.1 %collective-permute-start.1 = (bf16[64,4224]{1,0:T(8,128)(2,1)S(1)}, bf16[64,4224]{1,0:T(8,128)(2,1)S(1)}, u32[]{:S(2)}, u32[]{:S(2)}) collective-permute-start(bf16[64,4224]{1,0:T(8,128)(2,1)S(1)} %get-tuple-element.12.own.refs_1_), channel_id=1, source_target_pairs={{4,0},{2,1},{1,2},{0,3},{7,4},{6,5},{5,6},{3,7},{12,8},{10,9},{11,... | collective-permute-start | bytes 1622024 | tf_op jit(solution)/shard_map/ppermute | solution.py:164
  13.7 1.9 %collective-permute-start.3 = (bf16[64,4224]{1,0:T(8,128)(2,1)S(1)}, bf16[64,4224]{1,0:T(8,128)(2,1)S(1)}, u32[]{:S(2)}, u32[]{:S(2)}) collective-permute-start(bf16[64,4224]{1,0:T(8,128)(2,1)S(1)} %get-tuple-element.12.own.refs_1_), channel_id=1, source_target_pairs={{12,0},{5,1},{14,2},{15,3},{0,4},{4,5},{7,6},{11,7},{9,8},{8,9},{6... | collective-permute-start | bytes 1622024 | tf_op jit(solution)/shard_map/ppermute | solution.py:164
  15.6 0.0 collective-permute-done.first.refs_2_
  15.7 1.8 %collective-permute-done.2.second.refs_4_ = bf16[64,4224]{1,0:T(8,128)(2,1)S(1)} collective-permute-done((bf16[64,4224]{1,0:T(8,128)(2,1)S(1)}, bf16[64,4224]{1,0:T(8,128)(2,1)S(1)}, u32[]{:S(2)}, u32[]{:S(2)}) %collective-permute-start.2) | collective-permute-done | bytes 540704 | tf_op jit(solution)/shard_map/ppermute | solution.py:164
  17.5 0.1 choose.2
  17.6 7.0 %collective-permute-start.4 = (bf16[64,4224]{1,0:T(8,128)(2,1)S(1)}, bf16[64,4224]{1,0:T(8,128)(2,1)S(1)}, u32[]{:S(2)}, u32[]{:S(2)}) collective-permute-start(bf16[64,4224]{1,0:T(8,128)(2,1)S(1)} %get-tuple-element.13), channel_id=1, source_target_pairs={{1,0},{0,1},{3,2},{2,3},{8,4},{4,5},{7,6},{11,7},{12,8},{5,9},{6,1... | collective-permute-start | bytes 1622024 | tf_op jit(solution)/shard_map/ppermute | solution.py:175
  24.6 1.9 %collective-permute-start.5 = (bf16[64,4224]{1,0:T(8,128)(2,1)S(1)}, bf16[64,4224]{1,0:T(8,128)(2,1)S(1)}, u32[]{:S(2)}, u32[]{:S(2)}) collective-permute-start(bf16[64,4224]{1,0:T(8,128)(2,1)S(1)} %get-tuple-element.14), channel_id=1, source_target_pairs={{12,0},{5,1},{6,2},{0,3},{7,4},{9,5},{2,6},{3,7},{4,8},{10,9},{14,... | collective-permute-start | bytes 1622024 | tf_op jit(solution)/shard_map/ppermute | solution.py:175
  26.5 0.0 collective-permute-done.1.first.refs_3_
  26.5 0.1 choose.3
  26.6 8.4 %collective-permute-start.6 = (bf16[64,4224]{1,0:T(8,128)(2,1)S(1)}, bf16[64,4224]{1,0:T(8,128)(2,1)S(1)}, u32[]{:S(2)}, u32[]{:S(2)}) collective-permute-start(bf16[64,4224]{1,0:T(8,128)(2,1)S(1)} %get-tuple-element.15), channel_id=1, source_target_pairs={{1,0},{0,1},{3,2},{2,3},{8,4},{4,5},{7,6},{11,7},{12,8},{5,9},{6,1... | collective-permute-start | bytes 1622024 | tf_op jit(solution)/shard_map/ppermute | solution.py:175
  35.1 1.9 %collective-permute-start.7 = (bf16[64,4224]{1,0:T(8,128)(2,1)S(1)}, bf16[64,4224]{1,0:T(8,128)(2,1)S(1)}, u32[]{:S(2)}, u32[]{:S(2)}) collective-permute-start(bf16[64,4224]{1,0:T(8,128)(2,1)S(1)} %get-tuple-element.16), channel_id=1, source_target_pairs={{12,0},{5,1},{6,2},{0,3},{7,4},{9,5},{2,6},{3,7},{4,8},{10,9},{14,... | collective-permute-start | bytes 1622024 | tf_op jit(solution)/shard_map/ppermute | solution.py:175
  37.0 2.0 %meet_kernel.2.refs_8_ = f32[8,384]{1,0:T(8,128)S(1)} custom-call(bf16[64,4224]{1,0:T(8,128)(2,1)S(1)} %get-tuple-element.11.own.refs_0_, bf16[64,4224]{1,0:T(8,128)(2,1)S(1)} %get-tuple-element.12.own.refs_1_, bf16[64,4224]{1,0:T(8,128)(2,1)S(1)} %collective-permute-done.first.refs_2_, bf16[64,4224]{1,0:T(8,128)(2,1)S(1)} %collective-permute-done.1.first.refs_3_, ...), custom_call_target="tpu_custom_call" | custom-call | flops 1207959552 | bytes 3145728 | tf_op jit(solution)/shard_map/meet_kernel/pallas_call | solution.py:146
  39.0 1.7 %meet_kernel.3.refs_10_ = f32[8,512]{1,0:T(8,128)S(1)} custom-call(bf16[64,4224]{1,0:T(8,128)(2,1)S(1)} %get-tuple-element.11.own.refs_0_, bf16[64,4224]{1,0:T(8,128)(2,1)S(1)} %get-tuple-element.12.own.refs_1_, bf16[64,4224]{1,0:T(8,128)(2,1)S(1)} %collective-permute-done.first.refs_2_, bf16[64,4224]{1,0:T(8,128)(2,1)S(1)} %collective-permute-done.1.first.refs_3_, ...), custom_call_target="tpu_custom_call" | custom-call | flops 536870912 | bytes 4194304 | tf_op jit(solution)/shard_map/meet_kernel/pallas_call | solution.py:146
  40.7 1.7 %collective-permute-done.6.refs_8_ = bf16[64,4224]{1,0:T(8,128)(2,1)S(1)} collective-permute-done((bf16[64,4224]{1,0:T(8,128)(2,1)S(1)}, bf16[64,4224]{1,0:T(8,128)(2,1)S(1)}, u32[]{:S(2)}, u32[]{:S(2)}) %collective-permute-start.6) | collective-permute-done | bytes 540704 | tf_op jit(solution)/shard_map/ppermute | solution.py:175
  42.4 3.9 %collective-permute-done.7.refs_9_ = bf16[64,4224]{1,0:T(8,128)(2,1)S(1)} collective-permute-done((bf16[64,4224]{1,0:T(8,128)(2,1)S(1)}, bf16[64,4224]{1,0:T(8,128)(2,1)S(1)}, u32[]{:S(2)}, u32[]{:S(2)}) %collective-permute-start.7) | collective-permute-done | bytes 540704 | tf_op jit(solution)/shard_map/ppermute | solution.py:175
  46.3 1.9 %last_kernel.1 = f32[16,128]{1,0:T(8,128)S(1)} custom-call(bf16[64,4224]{1,0:T(8,128)(2,1)S(1)} %get-tuple-element.11.own.refs_0_, bf16[64,4224]{1,0:T(8,128)(2,1)S(1)} %get-tuple-element.12.own.refs_1_, bf16[64,4224]{1,0:T(8,128)(2,1)S(1)} %collective-permute-done.first.refs_2_, bf16[64,4224]{1,0:T(8,128)(2,1)S(1)} %collective-permute-done.1.first.refs_3_, ...), custom_call_target="tpu_custom_call" | custom-call | flops 671088640 | bytes 5242880 | tf_op jit(solution)/shard_map/last_kernel/pallas_call | solution.py:146
  48.3 12.5 %all_to_all.9 = f32[16,1,128]{2,1,0:T(1,128)S(1)} all-to-all(f32[16,1,128]{2,1,0:T(1,128)S(1)} %bitcast.5), channel_id=1, replica_groups=mesh['shard'=32,'grp'=16] {'grp'}, dimensions={0} | all-to-all | bytes 16384 | tf_op jit(solution)/shard_map/all_to_all | solution.py:180
  60.7 0.5 reduce_max.9
  (7 shorter events, 0.0 us)
Async XLA Ops:
  0.0 0.7 %copy-start.1 = (s32[128]{0:T(128)S(1)}, s32[128]{0:T(128)}, u32[]{:S(2)}) copy-start(s32[128]{0:T(128)} %param.5) | copy-start | bytes 1540
  0.0 0.7 %copy-start.2 = (s32[128]{0:T(128)S(1)}, s32[128]{0:T(128)}, u32[]{:S(2)}) copy-start(s32[128]{0:T(128)} %param.4) | copy-start | bytes 1540
  0.7 1.2 %copy-start = (bf16[128,4096]{1,0:T(8,128)(2,1)S(1)}, bf16[128,4096]{1,0:T(8,128)(2,1)}, u32[]{:S(2)}) copy-start(bf16[128,4096]{1,0:T(8,128)(2,1)} %emb.1) | copy-start | bytes 3145732
  2.3 13.4 %collective-permute-start = (bf16[64,4224]{1,0:T(8,128)(2,1)S(1)}, bf16[64,4224]{1,0:T(8,128)(2,1)S(1)}, u32[]{:S(2)}, u32[]{:S(2)}) collective-permute-start(bf16[64,4224]{1,0:T(8,128)(2,1)S(1)} %get-tuple-element.11.own.refs_0_), channel_id=1, source_target_pairs={{4,0},{2,1},{1,2},{0,3},{7,4},{6,5},{5,6},{3,7},{12,8},{10,9},{11,... | collective-permute-start | bytes 1622024 | tf_op jit(solution)/shard_map/ppermute | solution.py:164
  5.7 11.8 %collective-permute-start.2 = (bf16[64,4224]{1,0:T(8,128)(2,1)S(1)}, bf16[64,4224]{1,0:T(8,128)(2,1)S(1)}, u32[]{:S(2)}, u32[]{:S(2)}) collective-permute-start(bf16[64,4224]{1,0:T(8,128)(2,1)S(1)} %get-tuple-element.11.own.refs_0_), channel_id=1, source_target_pairs={{12,0},{5,1},{14,2},{15,3},{0,4},{4,5},{7,6},{11,7},{9,8},{8,9},{6... | collective-permute-start | bytes 1622024 | tf_op jit(solution)/shard_map/ppermute | solution.py:164
  10.6 15.9 %collective-permute-start.1 = (bf16[64,4224]{1,0:T(8,128)(2,1)S(1)}, bf16[64,4224]{1,0:T(8,128)(2,1)S(1)}, u32[]{:S(2)}, u32[]{:S(2)}) collective-permute-start(bf16[64,4224]{1,0:T(8,128)(2,1)S(1)} %get-tuple-element.12.own.refs_1_), channel_id=1, source_target_pairs={{4,0},{2,1},{1,2},{0,3},{7,4},{6,5},{5,6},{3,7},{12,8},{10,9},{11,... | collective-permute-start | bytes 1622024 | tf_op jit(solution)/shard_map/ppermute | solution.py:164
  13.7 12.8 %collective-permute-start.3 = (bf16[64,4224]{1,0:T(8,128)(2,1)S(1)}, bf16[64,4224]{1,0:T(8,128)(2,1)S(1)}, u32[]{:S(2)}, u32[]{:S(2)}) collective-permute-start(bf16[64,4224]{1,0:T(8,128)(2,1)S(1)} %get-tuple-element.12.own.refs_1_), channel_id=1, source_target_pairs={{12,0},{5,1},{14,2},{15,3},{0,4},{4,5},{7,6},{11,7},{9,8},{8,9},{6... | collective-permute-start | bytes 1622024 | tf_op jit(solution)/shard_map/ppermute | solution.py:164
  17.6 21.5 %collective-permute-start.4 = (bf16[64,4224]{1,0:T(8,128)(2,1)S(1)}, bf16[64,4224]{1,0:T(8,128)(2,1)S(1)}, u32[]{:S(2)}, u32[]{:S(2)}) collective-permute-start(bf16[64,4224]{1,0:T(8,128)(2,1)S(1)} %get-tuple-element.13), channel_id=1, source_target_pairs={{1,0},{0,1},{3,2},{2,3},{8,4},{4,5},{7,6},{11,7},{12,8},{5,9},{6,1... | collective-permute-start | bytes 1622024 | tf_op jit(solution)/shard_map/ppermute | solution.py:175
  24.6 14.5 %collective-permute-start.5 = (bf16[64,4224]{1,0:T(8,128)(2,1)S(1)}, bf16[64,4224]{1,0:T(8,128)(2,1)S(1)}, u32[]{:S(2)}, u32[]{:S(2)}) collective-permute-start(bf16[64,4224]{1,0:T(8,128)(2,1)S(1)} %get-tuple-element.14), channel_id=1, source_target_pairs={{12,0},{5,1},{6,2},{0,3},{7,4},{9,5},{2,6},{3,7},{4,8},{10,9},{14,... | collective-permute-start | bytes 1622024 | tf_op jit(solution)/shard_map/ppermute | solution.py:175
  26.6 15.8 %collective-permute-start.6 = (bf16[64,4224]{1,0:T(8,128)(2,1)S(1)}, bf16[64,4224]{1,0:T(8,128)(2,1)S(1)}, u32[]{:S(2)}, u32[]{:S(2)}) collective-permute-start(bf16[64,4224]{1,0:T(8,128)(2,1)S(1)} %get-tuple-element.15), channel_id=1, source_target_pairs={{1,0},{0,1},{3,2},{2,3},{8,4},{4,5},{7,6},{11,7},{12,8},{5,9},{6,1... | collective-permute-start | bytes 1622024 | tf_op jit(solution)/shard_map/ppermute | solution.py:175
  35.1 11.3 %collective-permute-start.7 = (bf16[64,4224]{1,0:T(8,128)(2,1)S(1)}, bf16[64,4224]{1,0:T(8,128)(2,1)S(1)}, u32[]{:S(2)}, u32[]{:S(2)}) collective-permute-start(bf16[64,4224]{1,0:T(8,128)(2,1)S(1)} %get-tuple-element.16), channel_id=1, source_target_pairs={{12,0},{5,1},{6,2},{0,3},{7,4},{9,5},{2,6},{3,7},{4,8},{10,9},{14,... | collective-permute-start | bytes 1622024 | tf_op jit(solution)/shard_map/ppermute | solution.py:175

commit v4 on v3

--- a/solution.py
+++ b/solution.py
@@ -11,20 +11,20 @@
 
 ROUTE = (
     (
+        (1, 0, 3, 2, 5, 9, 10, 6, 4, 13, 14, 7, 8, 12, 15, 11),
+        (3, 13, 6, 7, 8, 1, 2, 4, 11, 5, 9, 15, 0, 14, 10, 12),
+        (3, 2, 1, 7, 0, 6, 5, 4, 9, 13, 11, 10, 8, 14, 15, 12),
+        (4, 13, 14, 15, 5, 1, 10, 6, 11, 8, 9, 7, 0, 12, 2, 3),
+        (2, 0, 2, 2, 2, 0, 2, 2, 1, 1, 2, 1, 1, 1, 2, 1),
+        (1, 1, 1, 1, 1, 1, 1, 1, 2, 1, 1, 2, 1, 1, 2, 2),
+    ),
+    (
         (4, 2, 1, 0, 7, 6, 5, 3, 12, 10, 11, 8, 15, 9, 13, 14),
         (12, 5, 14, 15, 0, 4, 7, 11, 9, 8, 6, 10, 13, 1, 2, 3),
         (1, 0, 3, 2, 8, 4, 7, 11, 12, 5, 6, 15, 13, 9, 10, 14),
         (12, 5, 6, 0, 7, 9, 2, 3, 4, 10, 14, 8, 15, 1, 13, 11),
         (2, 0, 0, 0, 2, 2, 1, 1, 2, 2, 0, 2, 2, 1, 2, 1),
         (1, 2, 2, 2, 1, 1, 2, 2, 1, 2, 2, 1, 0, 1, 1, 2),
-    ),
-    (
-        (1, 0, 3, 2, 5, 9, 10, 6, 4, 13, 14, 7, 8, 12, 15, 11),
-        (3, 13, 6, 7, 8, 1, 2, 4, 11, 5, 9, 15, 0, 14, 10, 12),
-        (3, 2, 1, 7, 0, 6, 5, 4, 9, 13, 11, 10, 8, 14, 15, 12),
-        (4, 13, 14, 15, 5, 1, 10, 6, 11, 8, 9, 7, 0, 12, 2, 3),
-        (2, 0, 2, 2, 2, 0, 2, 2, 1, 1, 2, 1, 1, 1, 2, 1),
-        (1, 1, 1, 1, 1, 1, 1, 1, 2, 1, 1, 2, 1, 1, 2, 2),
     ),
 )
 

time: 61.7 us -> 58.4 us (0.947)
  starting transfers between devices: 32.6 us -> 23.4 us
  waiting for transfers between devices: 7.41 us -> 14.8 us
  blocking collectives: 12.5 us -> 11.1 us
    ppermute x4, starting transfers between devices: 19.3 us -> 9.34 us  [body(): came.append([lax.ppermute(passed[k], axes, pairs(2 + k)) for k in (0, 1)])]
    ppermute x4, waiting for transfers between devices: 1.81 us -> 8 us  [body(): lax.ppermute(own[i], axes, pairs(k))]
    all_to_all x1, blocking collectives: 12.5 us -> 11.1 us  [body(): given = lax.all_to_all(table, 'grp', 0, 0, tiled=True)]
    ppermute x4, waiting for transfers between devices: 5.61 us -> 6.82 us  [body(): came.append([lax.ppermute(passed[k], axes, pairs(2 + k)) for k in (0, 1)])]
    ppermute x4, starting transfers between devices: 13.3 us -> 14.1 us  [body(): lax.ppermute(own[i], axes, pairs(k))]
  transfers between devices with their start and end apart: 8 -> 8, of which waited for: 3 -> 6; matrix products, arithmetic and copies ran while one was open for 0% -> 0% of each run, Pallas kernels for 6% -> 7%
where the time goes in v4:
time: 58.4 us; the launch traced here: 58.1 us
  starting transfers between devices  23.4 us (40%)
  waiting for transfers between devices  14.8 us (25%)
  blocking collectives  11.1 us (19%)
  Pallas kernels  6.14 us (11%)
  local copies, waits for them, and re-layouts  1.89 us (3%)
    ppermute x4, starting transfers between devices, body(): lax.ppermute(own[i], axes, pairs(k))  14.1 us
    all_to_all x1, blocking collectives, body(): given = lax.all_to_all(table, 'grp', 0, 0, tiled=True)  11.1 us
    ppermute x4, starting transfers between devices, body(): came.append([lax.ppermute(passed[k], axes, pairs(2 + k)) for k in (0, 1)])  9.34 us
    ppermute x4, waiting for transfers between devices, body(): lax.ppermute(own[i], axes, pairs(k))  8 us
    ppermute x4, waiting for transfers between devices, body(): came.append([lax.ppermute(passed[k], axes, pairs(2 + k)) for k in (0, 1)])  6.82 us
    pallas_call x3, Pallas kernels, meet_call(): pl.pallas_call(functools.partial(kernel, len(blocks), count), out_shape=j...  5.6 us
    unnamed x6, local copies, waits for them, and re-layouts  1.89 us
  transfers between devices with their start and end apart: 8, of which 6 were waited for; matrix products, arithmetic and copies ran while one was open for 0% of the time, Pallas kernels for 7%

profile of v4, /device:TPU:2, one launch (start us, length us, event | category | flops | bytes accessed | tf_op | source)
XLA Modules:
  0.0 58.1 jit_solution(4620621370726407713)
XLA Ops:
  0.0 0.7 %copy-done.1 = s32[128]{0:T(128)S(1)} copy-done((s32[128]{0:T(128)S(1)}, s32[128]{0:T(128)}, u32[]{:S(2)}) %copy-start.1) | copy-done | bytes 536
  0.7 1.2 %copy-done = bf16[128,4096]{1,0:T(8,128)(2,1)S(1)} copy-done((bf16[128,4096]{1,0:T(8,128)(2,1)S(1)}, bf16[128,4096]{1,0:T(8,128)(2,1)}, u32[]{:S(2)}) %copy-start) | copy-done | bytes 1048600
  1.9 0.4 pack.1
  2.3 7.8 %collective-permute-start = (bf16[64,4224]{1,0:T(8,128)(2,1)S(1)}, bf16[64,4224]{1,0:T(8,128)(2,1)S(1)}, u32[]{:S(2)}, u32[]{:S(2)}) collective-permute-start(bf16[64,4224]{1,0:T(8,128)(2,1)S(1)} %get-tuple-element.11.own.refs_0_), channel_id=1, source_target_pairs={{1,0},{0,1},{3,2},{2,3},{5,4},{9,5},{10,6},{6,7},{4,8},{13,9},{14,... | collective-permute-start | bytes 1622024 | tf_op jit(solution)/shard_map/ppermute | solution.py:164
  10.1 1.9 %collective-permute-start.2 = (bf16[64,4224]{1,0:T(8,128)(2,1)S(1)}, bf16[64,4224]{1,0:T(8,128)(2,1)S(1)}, u32[]{:S(2)}, u32[]{:S(2)}) collective-permute-start(bf16[64,4224]{1,0:T(8,128)(2,1)S(1)} %get-tuple-element.11.own.refs_0_), channel_id=1, source_target_pairs={{3,0},{13,1},{6,2},{7,3},{8,4},{1,5},{2,6},{4,7},{11,8},{5,9},{9,1... | collective-permute-start | bytes 1622024 | tf_op jit(solution)/shard_map/ppermute | solution.py:164
  12.0 1.9 %collective-permute-start.1 = (bf16[64,4224]{1,0:T(8,128)(2,1)S(1)}, bf16[64,4224]{1,0:T(8,128)(2,1)S(1)}, u32[]{:S(2)}, u32[]{:S(2)}) collective-permute-start(bf16[64,4224]{1,0:T(8,128)(2,1)S(1)} %get-tuple-element.12.own.refs_1_), channel_id=1, source_target_pairs={{1,0},{0,1},{3,2},{2,3},{5,4},{9,5},{10,6},{6,7},{4,8},{13,9},{14,... | collective-permute-start | bytes 1622024 | tf_op jit(solution)/shard_map/ppermute | solution.py:164
  13.9 2.4 %collective-permute-start.3 = (bf16[64,4224]{1,0:T(8,128)(2,1)S(1)}, bf16[64,4224]{1,0:T(8,128)(2,1)S(1)}, u32[]{:S(2)}, u32[]{:S(2)}) collective-permute-start(bf16[64,4224]{1,0:T(8,128)(2,1)S(1)} %get-tuple-element.12.own.refs_1_), channel_id=1, source_target_pairs={{3,0},{13,1},{6,2},{7,3},{8,4},{1,5},{2,6},{4,7},{11,8},{5,9},{9,1... | collective-permute-start | bytes 1622024 | tf_op jit(solution)/shard_map/ppermute | solution.py:164
  16.4 1.0 %collective-permute-done.first.refs_2_ = bf16[64,4224]{1,0:T(8,128)(2,1)S(1)} collective-permute-done((bf16[64,4224]{1,0:T(8,128)(2,1)S(1)}, bf16[64,4224]{1,0:T(8,128)(2,1)S(1)}, u32[]{:S(2)}, u32[]{:S(2)}) %collective-permute-start) | collective-permute-done | bytes 540704 | tf_op jit(solution)/shard_map/ppermute | solution.py:164
  17.4 5.1 %collective-permute-done.2.second.refs_4_ = bf16[64,4224]{1,0:T(8,128)(2,1)S(1)} collective-permute-done((bf16[64,4224]{1,0:T(8,128)(2,1)S(1)}, bf16[64,4224]{1,0:T(8,128)(2,1)S(1)}, u32[]{:S(2)}, u32[]{:S(2)}) %collective-permute-start.2) | collective-permute-done | bytes 540704 | tf_op jit(solution)/shard_map/ppermute | solution.py:164
  22.5 0.1 choose.2
  22.7 1.9 %collective-permute-start.4 = (bf16[64,4224]{1,0:T(8,128)(2,1)S(1)}, bf16[64,4224]{1,0:T(8,128)(2,1)S(1)}, u32[]{:S(2)}, u32[]{:S(2)}) collective-permute-start(bf16[64,4224]{1,0:T(8,128)(2,1)S(1)} %get-tuple-element.13), channel_id=1, source_target_pairs={{3,0},{2,1},{1,2},{7,3},{0,4},{6,5},{5,6},{4,7},{9,8},{13,9},{11,1... | collective-permute-start | bytes 1622024 | tf_op jit(solution)/shard_map/ppermute | solution.py:175
  24.6 1.9 %collective-permute-start.5 = (bf16[64,4224]{1,0:T(8,128)(2,1)S(1)}, bf16[64,4224]{1,0:T(8,128)(2,1)S(1)}, u32[]{:S(2)}, u32[]{:S(2)}) collective-permute-start(bf16[64,4224]{1,0:T(8,128)(2,1)S(1)} %get-tuple-element.14), channel_id=1, source_target_pairs={{4,0},{13,1},{14,2},{15,3},{5,4},{1,5},{10,6},{6,7},{11,8},{8,9},{... | collective-permute-start | bytes 1622024 | tf_op jit(solution)/shard_map/ppermute | solution.py:175
  26.5 1.8 %collective-permute-done.3.second.refs_5_ = bf16[64,4224]{1,0:T(8,128)(2,1)S(1)} collective-permute-done((bf16[64,4224]{1,0:T(8,128)(2,1)S(1)}, bf16[64,4224]{1,0:T(8,128)(2,1)S(1)}, u32[]{:S(2)}, u32[]{:S(2)}) %collective-permute-start.3) | collective-permute-done | bytes 540704 | tf_op jit(solution)/shard_map/ppermute | solution.py:164
  28.3 0.1 choose.3
  28.4 3.6 %collective-permute-start.6 = (bf16[64,4224]{1,0:T(8,128)(2,1)S(1)}, bf16[64,4224]{1,0:T(8,128)(2,1)S(1)}, u32[]{:S(2)}, u32[]{:S(2)}) collective-permute-start(bf16[64,4224]{1,0:T(8,128)(2,1)S(1)} %get-tuple-element.15), channel_id=1, source_target_pairs={{3,0},{2,1},{1,2},{7,3},{0,4},{6,5},{5,6},{4,7},{9,8},{13,9},{11,1... | collective-permute-start | bytes 1622024 | tf_op jit(solution)/shard_map/ppermute | solution.py:175
  32.0 1.9 %collective-permute-start.7 = (bf16[64,4224]{1,0:T(8,128)(2,1)S(1)}, bf16[64,4224]{1,0:T(8,128)(2,1)S(1)}, u32[]{:S(2)}, u32[]{:S(2)}) collective-permute-start(bf16[64,4224]{1,0:T(8,128)(2,1)S(1)} %get-tuple-element.16), channel_id=1, source_target_pairs={{4,0},{13,1},{14,2},{15,3},{5,4},{1,5},{10,6},{6,7},{11,8},{8,9},{... | collective-permute-start | bytes 1622024 | tf_op jit(solution)/shard_map/ppermute | solution.py:175
  34.0 2.0 %meet_kernel.2.refs_8_ = f32[8,384]{1,0:T(8,128)S(1)} custom-call(bf16[64,4224]{1,0:T(8,128)(2,1)S(1)} %get-tuple-element.11.own.refs_0_, bf16[64,4224]{1,0:T(8,128)(2,1)S(1)} %get-tuple-element.12.own.refs_1_, bf16[64,4224]{1,0:T(8,128)(2,1)S(1)} %collective-permute-done.first.refs_2_, bf16[64,4224]{1,0:T(8,128)(2,1)S(1)} %collective-permute-done.1.first.refs_3_, ...), custom_call_target="tpu_custom_call" | custom-call | flops 1207959552 | bytes 3145728 | tf_op jit(solution)/shard_map/meet_kernel/pallas_call | solution.py:146
  36.0 1.1 %collective-permute-done.5.refs_7_ = bf16[64,4224]{1,0:T(8,128)(2,1)S(1)} collective-permute-done((bf16[64,4224]{1,0:T(8,128)(2,1)S(1)}, bf16[64,4224]{1,0:T(8,128)(2,1)S(1)}, u32[]{:S(2)}, u32[]{:S(2)}) %collective-permute-start.5) | collective-permute-done | bytes 540704 | tf_op jit(solution)/shard_map/ppermute | solution.py:175
  37.0 1.7 %meet_kernel.3.refs_10_ = f32[8,512]{1,0:T(8,128)S(1)} custom-call(bf16[64,4224]{1,0:T(8,128)(2,1)S(1)} %get-tuple-element.11.own.refs_0_, bf16[64,4224]{1,0:T(8,128)(2,1)S(1)} %get-tuple-element.12.own.refs_1_, bf16[64,4224]{1,0:T(8,128)(2,1)S(1)} %collective-permute-done.first.refs_2_, bf16[64,4224]{1,0:T(8,128)(2,1)S(1)} %collective-permute-done.1.first.refs_3_, ...), custom_call_target="tpu_custom_call" | custom-call | flops 536870912 | bytes 4194304 | tf_op jit(solution)/shard_map/meet_kernel/pallas_call | solution.py:146
  38.8 0.9 %collective-permute-done.6.refs_8_ = bf16[64,4224]{1,0:T(8,128)(2,1)S(1)} collective-permute-done((bf16[64,4224]{1,0:T(8,128)(2,1)S(1)}, bf16[64,4224]{1,0:T(8,128)(2,1)S(1)}, u32[]{:S(2)}, u32[]{:S(2)}) %collective-permute-start.6) | collective-permute-done | bytes 540704 | tf_op jit(solution)/shard_map/ppermute | solution.py:175
  39.7 4.8 %collective-permute-done.7.refs_9_ = bf16[64,4224]{1,0:T(8,128)(2,1)S(1)} collective-permute-done((bf16[64,4224]{1,0:T(8,128)(2,1)S(1)}, bf16[64,4224]{1,0:T(8,128)(2,1)S(1)}, u32[]{:S(2)}, u32[]{:S(2)}) %collective-permute-start.7) | collective-permute-done | bytes 540704 | tf_op jit(solution)/shard_map/ppermute | solution.py:175
  44.5 1.9 %last_kernel.1 = f32[16,128]{1,0:T(8,128)S(1)} custom-call(bf16[64,4224]{1,0:T(8,128)(2,1)S(1)} %get-tuple-element.11.own.refs_0_, bf16[64,4224]{1,0:T(8,128)(2,1)S(1)} %get-tuple-element.12.own.refs_1_, bf16[64,4224]{1,0:T(8,128)(2,1)S(1)} %collective-permute-done.first.refs_2_, bf16[64,4224]{1,0:T(8,128)(2,1)S(1)} %collective-permute-done.1.first.refs_3_, ...), custom_call_target="tpu_custom_call" | custom-call | flops 671088640 | bytes 5242880 | tf_op jit(solution)/shard_map/last_kernel/pallas_call | solution.py:146
  46.4 11.1 %all_to_all.9 = f32[16,1,128]{2,1,0:T(1,128)S(1)} all-to-all(f32[16,1,128]{2,1,0:T(1,128)S(1)} %bitcast.5), channel_id=1, replica_groups=mesh['shard'=32,'grp'=16] {'grp'}, dimensions={0} | all-to-all | bytes 16384 | tf_op jit(solution)/shard_map/all_to_all | solution.py:180
  57.5 0.5 reduce_max.9
  (7 shorter events, 0.0 us)
Async XLA Ops:
  0.0 0.7 %copy-start.1 = (s32[128]{0:T(128)S(1)}, s32[128]{0:T(128)}, u32[]{:S(2)}) copy-start(s32[128]{0:T(128)} %param.5) | copy-start | bytes 1540
  0.0 0.7 %copy-start.2 = (s32[128]{0:T(128)S(1)}, s32[128]{0:T(128)}, u32[]{:S(2)}) copy-start(s32[128]{0:T(128)} %param.4) | copy-start | bytes 1540
  0.7 1.2 %copy-start = (bf16[128,4096]{1,0:T(8,128)(2,1)S(1)}, bf16[128,4096]{1,0:T(8,128)(2,1)}, u32[]{:S(2)}) copy-start(bf16[128,4096]{1,0:T(8,128)(2,1)} %emb.1) | copy-start | bytes 3145732
  2.3 15.1 %collective-permute-start = (bf16[64,4224]{1,0:T(8,128)(2,1)S(1)}, bf16[64,4224]{1,0:T(8,128)(2,1)S(1)}, u32[]{:S(2)}, u32[]{:S(2)}) collective-permute-start(bf16[64,4224]{1,0:T(8,128)(2,1)S(1)} %get-tuple-element.11.own.refs_0_), channel_id=1, source_target_pairs={{1,0},{0,1},{3,2},{2,3},{5,4},{9,5},{10,6},{6,7},{4,8},{13,9},{14,... | collective-permute-start | bytes 1622024 | tf_op jit(solution)/shard_map/ppermute | solution.py:164
  10.1 12.5 %collective-permute-start.2 = (bf16[64,4224]{1,0:T(8,128)(2,1)S(1)}, bf16[64,4224]{1,0:T(8,128)(2,1)S(1)}, u32[]{:S(2)}, u32[]{:S(2)}) collective-permute-start(bf16[64,4224]{1,0:T(8,128)(2,1)S(1)} %get-tuple-element.11.own.refs_0_), channel_id=1, source_target_pairs={{3,0},{13,1},{6,2},{7,3},{8,4},{1,5},{2,6},{4,7},{11,8},{5,9},{9,1... | collective-permute-start | bytes 1622024 | tf_op jit(solution)/shard_map/ppermute | solution.py:164
  12.0 14.5 %collective-permute-start.1 = (bf16[64,4224]{1,0:T(8,128)(2,1)S(1)}, bf16[64,4224]{1,0:T(8,128)(2,1)S(1)}, u32[]{:S(2)}, u32[]{:S(2)}) collective-permute-start(bf16[64,4224]{1,0:T(8,128)(2,1)S(1)} %get-tuple-element.12.own.refs_1_), channel_id=1, source_target_pairs={{1,0},{0,1},{3,2},{2,3},{5,4},{9,5},{10,6},{6,7},{4,8},{13,9},{14,... | collective-permute-start | bytes 1622024 | tf_op jit(solution)/shard_map/ppermute | solution.py:164
  13.9 14.4 %collective-permute-start.3 = (bf16[64,4224]{1,0:T(8,128)(2,1)S(1)}, bf16[64,4224]{1,0:T(8,128)(2,1)S(1)}, u32[]{:S(2)}, u32[]{:S(2)}) collective-permute-start(bf16[64,4224]{1,0:T(8,128)(2,1)S(1)} %get-tuple-element.12.own.refs_1_), channel_id=1, source_target_pairs={{3,0},{13,1},{6,2},{7,3},{8,4},{1,5},{2,6},{4,7},{11,8},{5,9},{9,1... | collective-permute-start | bytes 1622024 | tf_op jit(solution)/shard_map/ppermute | solution.py:164
  22.7 13.3 %collective-permute-start.4 = (bf16[64,4224]{1,0:T(8,128)(2,1)S(1)}, bf16[64,4224]{1,0:T(8,128)(2,1)S(1)}, u32[]{:S(2)}, u32[]{:S(2)}) collective-permute-start(bf16[64,4224]{1,0:T(8,128)(2,1)S(1)} %get-tuple-element.13), channel_id=1, source_target_pairs={{3,0},{2,1},{1,2},{7,3},{0,4},{6,5},{5,6},{4,7},{9,8},{13,9},{11,1... | collective-permute-start | bytes 1622024 | tf_op jit(solution)/shard_map/ppermute | solution.py:175
  24.6 12.5 %collective-permute-start.5 = (bf16[64,4224]{1,0:T(8,128)(2,1)S(1)}, bf16[64,4224]{1,0:T(8,128)(2,1)S(1)}, u32[]{:S(2)}, u32[]{:S(2)}) collective-permute-start(bf16[64,4224]{1,0:T(8,128)(2,1)S(1)} %get-tuple-element.14), channel_id=1, source_target_pairs={{4,0},{13,1},{14,2},{15,3},{5,4},{1,5},{10,6},{6,7},{11,8},{8,9},{... | collective-permute-start | bytes 1622024 | tf_op jit(solution)/shard_map/ppermute | solution.py:175
  28.4 11.3 %collective-permute-start.6 = (bf16[64,4224]{1,0:T(8,128)(2,1)S(1)}, bf16[64,4224]{1,0:T(8,128)(2,1)S(1)}, u32[]{:S(2)}, u32[]{:S(2)}) collective-permute-start(bf16[64,4224]{1,0:T(8,128)(2,1)S(1)} %get-tuple-element.15), channel_id=1, source_target_pairs={{3,0},{2,1},{1,2},{7,3},{0,4},{6,5},{5,6},{4,7},{9,8},{13,9},{11,1... | collective-permute-start | bytes 1622024 | tf_op jit(solution)/shard_map/ppermute | solution.py:175
  32.0 12.5 %collective-permute-start.7 = (bf16[64,4224]{1,0:T(8,128)(2,1)S(1)}, bf16[64,4224]{1,0:T(8,128)(2,1)S(1)}, u32[]{:S(2)}, u32[]{:S(2)}) collective-permute-start(bf16[64,4224]{1,0:T(8,128)(2,1)S(1)} %get-tuple-element.16), channel_id=1, source_target_pairs={{4,0},{13,1},{14,2},{15,3},{5,4},{1,5},{10,6},{6,7},{11,8},{8,9},{... | collective-permute-start | bytes 1622024 | tf_op jit(solution)/shard_map/ppermute | solution.py:175

commit v5 on v4

--- a/solution.py
+++ b/solution.py
@@ -11,20 +11,20 @@
 
 ROUTE = (
     (
-        (1, 0, 3, 2, 5, 9, 10, 6, 4, 13, 14, 7, 8, 12, 15, 11),
-        (3, 13, 6, 7, 8, 1, 2, 4, 11, 5, 9, 15, 0, 14, 10, 12),
-        (3, 2, 1, 7, 0, 6, 5, 4, 9, 13, 11, 10, 8, 14, 15, 12),
-        (4, 13, 14, 15, 5, 1, 10, 6, 11, 8, 9, 7, 0, 12, 2, 3),
-        (2, 0, 2, 2, 2, 0, 2, 2, 1, 1, 2, 1, 1, 1, 2, 1),
-        (1, 1, 1, 1, 1, 1, 1, 1, 2, 1, 1, 2, 1, 1, 2, 2),
+        (4, 5, 3, 7, 0, 1, 2, 11, 9, 13, 6, 10, 8, 12, 15, 14),
+        (3, 0, 1, 15, 8, 6, 10, 4, 11, 5, 14, 7, 13, 9, 2, 12),
+        (3, 13, 1, 15, 8, 6, 7, 4, 11, 5, 9, 10, 0, 14, 2, 12),
+        (12, 0, 3, 7, 5, 4, 2, 6, 9, 10, 14, 15, 8, 1, 13, 11),
+        (2, 1, 1, 1, 1, 1, 1, 2, 1, 1, 1, 2, 1, 1, 0, 1),
+        (1, 1, 1, 1, 2, 2, 1, 1, 2, 2, 0, 1, 2, 2, 1, 2),
     ),
     (
-        (4, 2, 1, 0, 7, 6, 5, 3, 12, 10, 11, 8, 15, 9, 13, 14),
-        (12, 5, 14, 15, 0, 4, 7, 11, 9, 8, 6, 10, 13, 1, 2, 3),
-        (1, 0, 3, 2, 8, 4, 7, 11, 12, 5, 6, 15, 13, 9, 10, 14),
-        (12, 5, 6, 0, 7, 9, 2, 3, 4, 10, 14, 8, 15, 1, 13, 11),
-        (2, 0, 0, 0, 2, 2, 1, 1, 2, 2, 0, 2, 2, 1, 2, 1),
-        (1, 2, 2, 2, 1, 1, 2, 2, 1, 2, 2, 1, 0, 1, 1, 2),
+        (12, 2, 14, 0, 7, 9, 5, 6, 4, 10, 11, 8, 15, 1, 13, 3),
+        (1, 13, 6, 2, 5, 4, 7, 3, 12, 8, 9, 15, 0, 14, 10, 11),
+        (1, 2, 14, 0, 7, 9, 5, 11, 4, 13, 6, 8, 15, 12, 10, 3),
+        (4, 5, 6, 2, 0, 1, 10, 3, 12, 8, 11, 7, 13, 9, 15, 14),
+        (1, 2, 2, 0, 2, 1, 2, 2, 1, 1, 2, 1, 0, 1, 2, 2),
+        (2, 1, 2, 2, 1, 0, 2, 1, 2, 2, 1, 2, 2, 0, 0, 1),
     ),
 )
 

time: 58.4 us -> 56.8 us (0.973)
  waiting for transfers between devices: 14.8 us -> 7.17 us
  starting transfers between devices: 23.4 us -> 27.6 us
  blocking collectives: 11.1 us -> 12.9 us
    ppermute x4, starting transfers between devices: 9.34 us -> 14.2 us  [body(): came.append([lax.ppermute(passed[k], axes, pairs(2 + k)) for k in (0, 1)])]
    ppermute x4, waiting for transfers between devices: 8 us -> 3.69 us  [body(): lax.ppermute(own[i], axes, pairs(k))]
    ppermute x4, waiting for transfers between devices: 6.82 us -> 3.48 us  [body(): came.append([lax.ppermute(passed[k], axes, pairs(2 + k)) for k in (0, 1)])]
    all_to_all x1, blocking collectives: 11.1 us -> 12.9 us  [body(): given = lax.all_to_all(table, 'grp', 0, 0, tiled=True)]
    ppermute x4, starting transfers between devices: 14.1 us -> 13.3 us  [body(): lax.ppermute(own[i], axes, pairs(k))]
  transfers between devices with their start and end apart: 8 -> 8, of which waited for: 6 -> 3; matrix products, arithmetic and copies ran while one was open for 0% -> 0% of each run, Pallas kernels for 7% -> 7%
where the time goes in v5:
time: 56.8 us; the launch traced here: 56.4 us
  starting transfers between devices  27.6 us (49%)
  blocking collectives  12.9 us (23%)
  waiting for transfers between devices  7.17 us (13%)
  Pallas kernels  6.16 us (11%)
  local copies, waits for them, and re-layouts  1.89 us (3%)
    ppermute x4, starting transfers between devices, body(): came.append([lax.ppermute(passed[k], axes, pairs(2 + k)) for k in (0, 1)])  14.2 us
    ppermute x4, starting transfers between devices, body(): lax.ppermute(own[i], axes, pairs(k))  13.3 us
    all_to_all x1, blocking collectives, body(): given = lax.all_to_all(table, 'grp', 0, 0, tiled=True)  12.9 us
    pallas_call x3, Pallas kernels, meet_call(): pl.pallas_call(functools.partial(kernel, len(blocks), count), out_shape=j...  5.6 us
    ppermute x4, waiting for transfers between devices, body(): lax.ppermute(own[i], axes, pairs(k))  3.69 us
    ppermute x4, waiting for transfers between devices, body(): came.append([lax.ppermute(passed[k], axes, pairs(2 + k)) for k in (0, 1)])  3.48 us
    unnamed x6, local copies, waits for them, and re-layouts  1.89 us
  transfers between devices with their start and end apart: 8, of which 3 were waited for; matrix products, arithmetic and copies ran while one was open for 0% of the time, Pallas kernels for 7%

profile of v5, /device:TPU:2, one launch (start us, length us, event | category | flops | bytes accessed | tf_op | source)
XLA Modules:
  0.0 56.4 jit_solution(1394341764043812740)
XLA Ops:
  0.0 0.7 %copy-done.1 = s32[128]{0:T(128)S(1)} copy-done((s32[128]{0:T(128)S(1)}, s32[128]{0:T(128)}, u32[]{:S(2)}) %copy-start.1) | copy-done | bytes 536
  0.7 0.0 copy-done.2
  0.7 1.2 %copy-done = bf16[128,4096]{1,0:T(8,128)(2,1)S(1)} copy-done((bf16[128,4096]{1,0:T(8,128)(2,1)S(1)}, bf16[128,4096]{1,0:T(8,128)(2,1)}, u32[]{:S(2)}) %copy-start) | copy-done | bytes 1048600
  1.9 0.4 pack.1
  2.3 3.5 %collective-permute-start = (bf16[64,4224]{1,0:T(8,128)(2,1)S(1)}, bf16[64,4224]{1,0:T(8,128)(2,1)S(1)}, u32[]{:S(2)}, u32[]{:S(2)}) collective-permute-start(bf16[64,4224]{1,0:T(8,128)(2,1)S(1)} %get-tuple-element.11.own.refs_0_), channel_id=1, source_target_pairs={{4,0},{5,1},{3,2},{7,3},{0,4},{1,5},{2,6},{11,7},{9,8},{13,9},{6,1... | collective-permute-start | bytes 1622024 | tf_op jit(solution)/shard_map/ppermute | solution.py:164
  5.8 3.4 %collective-permute-start.2 = (bf16[64,4224]{1,0:T(8,128)(2,1)S(1)}, bf16[64,4224]{1,0:T(8,128)(2,1)S(1)}, u32[]{:S(2)}, u32[]{:S(2)}) collective-permute-start(bf16[64,4224]{1,0:T(8,128)(2,1)S(1)} %get-tuple-element.11.own.refs_0_), channel_id=1, source_target_pairs={{3,0},{0,1},{1,2},{15,3},{8,4},{6,5},{10,6},{4,7},{11,8},{5,9},{14... | collective-permute-start | bytes 1622024 | tf_op jit(solution)/shard_map/ppermute | solution.py:164
  9.2 2.5 %collective-permute-start.1 = (bf16[64,4224]{1,0:T(8,128)(2,1)S(1)}, bf16[64,4224]{1,0:T(8,128)(2,1)S(1)}, u32[]{:S(2)}, u32[]{:S(2)}) collective-permute-start(bf16[64,4224]{1,0:T(8,128)(2,1)S(1)} %get-tuple-element.12.own.refs_1_), channel_id=1, source_target_pairs={{4,0},{5,1},{3,2},{7,3},{0,4},{1,5},{2,6},{11,7},{9,8},{13,9},{6,1... | collective-permute-start | bytes 1622024 | tf_op jit(solution)/shard_map/ppermute | solution.py:164
  11.7 3.9 %collective-permute-start.3 = (bf16[64,4224]{1,0:T(8,128)(2,1)S(1)}, bf16[64,4224]{1,0:T(8,128)(2,1)S(1)}, u32[]{:S(2)}, u32[]{:S(2)}) collective-permute-start(bf16[64,4224]{1,0:T(8,128)(2,1)S(1)} %get-tuple-element.12.own.refs_1_), channel_id=1, source_target_pairs={{3,0},{0,1},{1,2},{15,3},{8,4},{6,5},{10,6},{4,7},{11,8},{5,9},{14... | collective-permute-start | bytes 1622024 | tf_op jit(solution)/shard_map/ppermute | solution.py:164
  15.6 0.0 collective-permute-done.first.refs_2_
  15.7 3.7 %collective-permute-done.2.second.refs_4_ = bf16[64,4224]{1,0:T(8,128)(2,1)S(1)} collective-permute-done((bf16[64,4224]{1,0:T(8,128)(2,1)S(1)}, bf16[64,4224]{1,0:T(8,128)(2,1)S(1)}, u32[]{:S(2)}, u32[]{:S(2)}) %collective-permute-start.2) | collective-permute-done | bytes 540704 | tf_op jit(solution)/shard_map/ppermute | solution.py:164
  19.3 0.1 choose.2
  19.4 1.9 %collective-permute-start.4 = (bf16[64,4224]{1,0:T(8,128)(2,1)S(1)}, bf16[64,4224]{1,0:T(8,128)(2,1)S(1)}, u32[]{:S(2)}, u32[]{:S(2)}) collective-permute-start(bf16[64,4224]{1,0:T(8,128)(2,1)S(1)} %get-tuple-element.13), channel_id=1, source_target_pairs={{3,0},{13,1},{1,2},{15,3},{8,4},{6,5},{7,6},{4,7},{11,8},{5,9},{9,... | collective-permute-start | bytes 1622024 | tf_op jit(solution)/shard_map/ppermute | solution.py:175
  21.4 5.1 %collective-permute-start.5 = (bf16[64,4224]{1,0:T(8,128)(2,1)S(1)}, bf16[64,4224]{1,0:T(8,128)(2,1)S(1)}, u32[]{:S(2)}, u32[]{:S(2)}) collective-permute-start(bf16[64,4224]{1,0:T(8,128)(2,1)S(1)} %get-tuple-element.14), channel_id=1, source_target_pairs={{12,0},{0,1},{3,2},{7,3},{5,4},{4,5},{2,6},{6,7},{9,8},{10,9},{14,... | collective-permute-start | bytes 1622024 | tf_op jit(solution)/shard_map/ppermute | solution.py:175
  26.5 0.0 collective-permute-done.1.first.refs_3_
  26.5 0.1 choose.3
  26.6 1.9 %collective-permute-start.6 = (bf16[64,4224]{1,0:T(8,128)(2,1)S(1)}, bf16[64,4224]{1,0:T(8,128)(2,1)S(1)}, u32[]{:S(2)}, u32[]{:S(2)}) collective-permute-start(bf16[64,4224]{1,0:T(8,128)(2,1)S(1)} %get-tuple-element.15), channel_id=1, source_target_pairs={{3,0},{13,1},{1,2},{15,3},{8,4},{6,5},{7,6},{4,7},{11,8},{5,9},{9,... | collective-permute-start | bytes 1622024 | tf_op jit(solution)/shard_map/ppermute | solution.py:175
  28.6 5.2 %collective-permute-start.7 = (bf16[64,4224]{1,0:T(8,128)(2,1)S(1)}, bf16[64,4224]{1,0:T(8,128)(2,1)S(1)}, u32[]{:S(2)}, u32[]{:S(2)}) collective-permute-start(bf16[64,4224]{1,0:T(8,128)(2,1)S(1)} %get-tuple-element.16), channel_id=1, source_target_pairs={{12,0},{0,1},{3,2},{7,3},{5,4},{4,5},{2,6},{6,7},{9,8},{10,9},{14,... | collective-permute-start | bytes 1622024 | tf_op jit(solution)/shard_map/ppermute | solution.py:175
  33.8 2.0 %meet_kernel.2.refs_8_ = f32[8,384]{1,0:T(8,128)S(1)} custom-call(bf16[64,4224]{1,0:T(8,128)(2,1)S(1)} %get-tuple-element.11.own.refs_0_, bf16[64,4224]{1,0:T(8,128)(2,1)S(1)} %get-tuple-element.12.own.refs_1_, bf16[64,4224]{1,0:T(8,128)(2,1)S(1)} %collective-permute-done.first.refs_2_, bf16[64,4224]{1,0:T(8,128)(2,1)S(1)} %collective-permute-done.1.first.refs_3_, ...), custom_call_target="tpu_custom_call" | custom-call | flops 1207959552 | bytes 3145728 | tf_op jit(solution)/shard_map/meet_kernel/pallas_call | solution.py:146
  35.8 1.7 %meet_kernel.3.refs_10_ = f32[8,512]{1,0:T(8,128)S(1)} custom-call(bf16[64,4224]{1,0:T(8,128)(2,1)S(1)} %get-tuple-element.11.own.refs_0_, bf16[64,4224]{1,0:T(8,128)(2,1)S(1)} %get-tuple-element.12.own.refs_1_, bf16[64,4224]{1,0:T(8,128)(2,1)S(1)} %collective-permute-done.first.refs_2_, bf16[64,4224]{1,0:T(8,128)(2,1)S(1)} %collective-permute-done.1.first.refs_3_, ...), custom_call_target="tpu_custom_call" | custom-call | flops 536870912 | bytes 4194304 | tf_op jit(solution)/shard_map/meet_kernel/pallas_call | solution.py:146
  37.6 1.7 %collective-permute-done.6.refs_8_ = bf16[64,4224]{1,0:T(8,128)(2,1)S(1)} collective-permute-done((bf16[64,4224]{1,0:T(8,128)(2,1)S(1)}, bf16[64,4224]{1,0:T(8,128)(2,1)S(1)}, u32[]{:S(2)}, u32[]{:S(2)}) %collective-permute-start.6) | collective-permute-done | bytes 540704 | tf_op jit(solution)/shard_map/ppermute | solution.py:175
  39.2 1.8 %collective-permute-done.7.refs_9_ = bf16[64,4224]{1,0:T(8,128)(2,1)S(1)} collective-permute-done((bf16[64,4224]{1,0:T(8,128)(2,1)S(1)}, bf16[64,4224]{1,0:T(8,128)(2,1)S(1)}, u32[]{:S(2)}, u32[]{:S(2)}) %collective-permute-start.7) | collective-permute-done | bytes 540704 | tf_op jit(solution)/shard_map/ppermute | solution.py:175
  41.0 1.9 %last_kernel.1 = f32[16,128]{1,0:T(8,128)S(1)} custom-call(bf16[64,4224]{1,0:T(8,128)(2,1)S(1)} %get-tuple-element.11.own.refs_0_, bf16[64,4224]{1,0:T(8,128)(2,1)S(1)} %get-tuple-element.12.own.refs_1_, bf16[64,4224]{1,0:T(8,128)(2,1)S(1)} %collective-permute-done.first.refs_2_, bf16[64,4224]{1,0:T(8,128)(2,1)S(1)} %collective-permute-done.1.first.refs_3_, ...), custom_call_target="tpu_custom_call" | custom-call | flops 671088640 | bytes 5242880 | tf_op jit(solution)/shard_map/last_kernel/pallas_call | solution.py:146
  42.9 12.9 %all_to_all.9 = f32[16,1,128]{2,1,0:T(1,128)S(1)} all-to-all(f32[16,1,128]{2,1,0:T(1,128)S(1)} %bitcast.5), channel_id=1, replica_groups=mesh['shard'=32,'grp'=16] {'grp'}, dimensions={0} | all-to-all | bytes 16384 | tf_op jit(solution)/shard_map/all_to_all | solution.py:180
  55.9 0.5 reduce_max.9
  (7 shorter events, 0.0 us)
Async XLA Ops:
  0.0 0.7 %copy-start.1 = (s32[128]{0:T(128)S(1)}, s32[128]{0:T(128)}, u32[]{:S(2)}) copy-start(s32[128]{0:T(128)} %param.5) | copy-start | bytes 1540
  0.0 0.7 %copy-start.2 = (s32[128]{0:T(128)S(1)}, s32[128]{0:T(128)}, u32[]{:S(2)}) copy-start(s32[128]{0:T(128)} %param.4) | copy-start | bytes 1540
  0.7 1.2 %copy-start = (bf16[128,4096]{1,0:T(8,128)(2,1)S(1)}, bf16[128,4096]{1,0:T(8,128)(2,1)}, u32[]{:S(2)}) copy-start(bf16[128,4096]{1,0:T(8,128)(2,1)} %emb.1) | copy-start | bytes 3145732
  2.3 13.4 %collective-permute-start = (bf16[64,4224]{1,0:T(8,128)(2,1)S(1)}, bf16[64,4224]{1,0:T(8,128)(2,1)S(1)}, u32[]{:S(2)}, u32[]{:S(2)}) collective-permute-start(bf16[64,4224]{1,0:T(8,128)(2,1)S(1)} %get-tuple-element.11.own.refs_0_), channel_id=1, source_target_pairs={{4,0},{5,1},{3,2},{7,3},{0,4},{1,5},{2,6},{11,7},{9,8},{13,9},{6,1... | collective-permute-start | bytes 1622024 | tf_op jit(solution)/shard_map/ppermute | solution.py:164
  5.8 13.6 %collective-permute-start.2 = (bf16[64,4224]{1,0:T(8,128)(2,1)S(1)}, bf16[64,4224]{1,0:T(8,128)(2,1)S(1)}, u32[]{:S(2)}, u32[]{:S(2)}) collective-permute-start(bf16[64,4224]{1,0:T(8,128)(2,1)S(1)} %get-tuple-element.11.own.refs_0_), channel_id=1, source_target_pairs={{3,0},{0,1},{1,2},{15,3},{8,4},{6,5},{10,6},{4,7},{11,8},{5,9},{14... | collective-permute-start | bytes 1622024 | tf_op jit(solution)/shard_map/ppermute | solution.py:164
  9.2 17.3 %collective-permute-start.1 = (bf16[64,4224]{1,0:T(8,128)(2,1)S(1)}, bf16[64,4224]{1,0:T(8,128)(2,1)S(1)}, u32[]{:S(2)}, u32[]{:S(2)}) collective-permute-start(bf16[64,4224]{1,0:T(8,128)(2,1)S(1)} %get-tuple-element.12.own.refs_1_), channel_id=1, source_target_pairs={{4,0},{5,1},{3,2},{7,3},{0,4},{1,5},{2,6},{11,7},{9,8},{13,9},{6,1... | collective-permute-start | bytes 1622024 | tf_op jit(solution)/shard_map/ppermute | solution.py:164
  11.7 14.8 %collective-permute-start.3 = (bf16[64,4224]{1,0:T(8,128)(2,1)S(1)}, bf16[64,4224]{1,0:T(8,128)(2,1)S(1)}, u32[]{:S(2)}, u32[]{:S(2)}) collective-permute-start(bf16[64,4224]{1,0:T(8,128)(2,1)S(1)} %get-tuple-element.12.own.refs_1_), channel_id=1, source_target_pairs={{3,0},{0,1},{1,2},{15,3},{8,4},{6,5},{10,6},{4,7},{11,8},{5,9},{14... | collective-permute-start | bytes 1622024 | tf_op jit(solution)/shard_map/ppermute | solution.py:164
  19.4 16.4 %collective-permute-start.4 = (bf16[64,4224]{1,0:T(8,128)(2,1)S(1)}, bf16[64,4224]{1,0:T(8,128)(2,1)S(1)}, u32[]{:S(2)}, u32[]{:S(2)}) collective-permute-start(bf16[64,4224]{1,0:T(8,128)(2,1)S(1)} %get-tuple-element.13), channel_id=1, source_target_pairs={{3,0},{13,1},{1,2},{15,3},{8,4},{6,5},{7,6},{4,7},{11,8},{5,9},{9,... | collective-permute-start | bytes 1622024 | tf_op jit(solution)/shard_map/ppermute | solution.py:175
  21.4 14.5 %collective-permute-start.5 = (bf16[64,4224]{1,0:T(8,128)(2,1)S(1)}, bf16[64,4224]{1,0:T(8,128)(2,1)S(1)}, u32[]{:S(2)}, u32[]{:S(2)}) collective-permute-start(bf16[64,4224]{1,0:T(8,128)(2,1)S(1)} %get-tuple-element.14), channel_id=1, source_target_pairs={{12,0},{0,1},{3,2},{7,3},{5,4},{4,5},{2,6},{6,7},{9,8},{10,9},{14,... | collective-permute-start | bytes 1622024 | tf_op jit(solution)/shard_map/ppermute | solution.py:175
  26.6 12.6 %collective-permute-start.6 = (bf16[64,4224]{1,0:T(8,128)(2,1)S(1)}, bf16[64,4224]{1,0:T(8,128)(2,1)S(1)}, u32[]{:S(2)}, u32[]{:S(2)}) collective-permute-start(bf16[64,4224]{1,0:T(8,128)(2,1)S(1)} %get-tuple-element.15), channel_id=1, source_target_pairs={{3,0},{13,1},{1,2},{15,3},{8,4},{6,5},{7,6},{4,7},{11,8},{5,9},{9,... | collective-permute-start | bytes 1622024 | tf_op jit(solution)/shard_map/ppermute | solution.py:175
  28.6 12.5 %collective-permute-start.7 = (bf16[64,4224]{1,0:T(8,128)(2,1)S(1)}, bf16[64,4224]{1,0:T(8,128)(2,1)S(1)}, u32[]{:S(2)}, u32[]{:S(2)}) collective-permute-start(bf16[64,4224]{1,0:T(8,128)(2,1)S(1)} %get-tuple-element.16), channel_id=1, source_target_pairs={{12,0},{0,1},{3,2},{7,3},{5,4},{4,5},{2,6},{6,7},{9,8},{10,9},{14,... | collective-permute-start | bytes 1622024 | tf_op jit(solution)/shard_map/ppermute | solution.py:175

commit v6 on v5

--- a/solution.py
+++ b/solution.py
@@ -8,6 +8,7 @@
 from jax.sharding import PartitionSpec as P
 
 META = 128
+FIRST = 80
 
 ROUTE = (
     (
@@ -53,13 +54,15 @@
     parts = jnp.where(row < 8, parts, lax.axis_index("grp")).astype(jnp.float32)
     wide = jnp.concatenate([parts, jnp.zeros((META - 16, rows), jnp.float32)], axis=0)
     meta = wide.T.astype(jnp.bfloat16)
-    half = rows // 2
-    for i, out in enumerate(outs):
-        out[:, width:] = meta[i * half : (i + 1) * half]
-        for at in range(0, half, 32):
-            block = emb[i * half + at : i * half + at + 32, :].astype(jnp.float32)
+    begin = 0
+    for out in outs:
+        count = out.shape[0]
+        out[:, width:] = meta[begin : begin + count]
+        for at in range(0, count, 16):
+            block = emb[begin + at : begin + at + 16, :].astype(jnp.float32)
             squares = jnp.sum(block * block, axis=1, keepdims=True)
-            out[at : at + 32, :width] = (block * lax.rsqrt(squares + 1e-06)).astype(jnp.bfloat16)
+            out[at : at + 16, :width] = (block * lax.rsqrt(squares + 1e-06)).astype(jnp.bfloat16)
+        begin += count
 
 
 def meet(blocks, count):
@@ -75,8 +78,8 @@
         return down
     across = jnp.where((ahead > 0) & (ahead < 2048), scores, -1.0)
     lanes = new.shape[0]
-    most = functools.reduce(jnp.maximum, [across[:, at : at + lanes] for at in range(0, across.shape[1], lanes)])
-    turned = jnp.max(most.T, axis=0, keepdims=True)
+    most = jnp.max(across, axis=1, keepdims=True)
+    turned = jnp.broadcast_to(most, (lanes, 128)).T[0:1]
     rest = jnp.full((1, down.shape[1] - lanes), -1.0, jnp.float32)
     return jnp.maximum(down, jnp.concatenate([rest, turned], axis=1))
 
@@ -92,13 +95,14 @@
 
 def last_kernel(number, count, *refs):
     blocks, before, out = refs[:number], refs[number], refs[-1]
-    half, width = blocks[0].shape[0], blocks[0].shape[1] - META
+    rows, width = blocks[0].shape[0] + blocks[1].shape[0], blocks[0].shape[1] - META
     best = meet(blocks, count)
     old = before.shape[1]
     best = jnp.concatenate([jnp.maximum(best[:, :old], before[0:1]), best[:, old:]], axis=1)
-    parts = [best[:, k * half : (k + 1) * half] for k in range(number)]
-    dest = lax.broadcasted_iota(jnp.int32, (16, 2 * half), 0).astype(jnp.float32)
-    total = jnp.full((16, 2 * half), -1.0, jnp.float32)
+    ends = [sum(b.shape[0] for b in blocks[: k + 1]) for k in range(number)]
+    parts = [best[:, end - b.shape[0] : end] for end, b in zip(ends, blocks)]
+    dest = lax.broadcasted_iota(jnp.int32, (16, rows), 0).astype(jnp.float32)
+    total = jnp.full((16, rows), -1.0, jnp.float32)
     for low, high in ((0, 1), (2, 3), (4, 5), (6, 8), (7, 9)):
         device = blocks[low][0:16, width:].astype(jnp.float32)[0:1, 8:9]
         value = jnp.concatenate([parts[low], parts[high]], axis=1)
@@ -137,25 +141,25 @@
 
     def body(embeddings, cluster_ids, order):
         rows, width = embeddings.shape
-        half = rows // 2
         f32 = jnp.float32
-        piece = jax.ShapeDtypeStruct((half, width + META), jnp.bfloat16)
+        pieces = [jax.ShapeDtypeStruct((n, width + META), jnp.bfloat16) for n in (FIRST, rows - FIRST)]
 
-        def meet_call(kernel, count, out, blocks, *before):
-            flops = 2 * len(blocks) * count * half * half * width
+        def meet_call(kernel, count, blocks, *before):
+            total, new = (sum(b.shape[0] for b in bs) for bs in (blocks, blocks[-count:]))
+            out = (n_grp, rows) if kernel is last_kernel else (8, total)
             return pl.pallas_call(
                 functools.partial(kernel, len(blocks), count),
                 out_shape=jax.ShapeDtypeStruct(out, f32),
                 in_specs=[vmem] * (len(blocks) + len(before)),
                 out_specs=vmem,
                 compiler_params=params,
-                cost_estimate=pl.CostEstimate(flops=flops, bytes_accessed=2 * len(blocks) * half * width, transcendentals=0),
+                cost_estimate=pl.CostEstimate(flops=2 * total * new * width, bytes_accessed=2 * total * width, transcendentals=0),
                 name=kernel.__name__,
             )(*blocks, *before)
 
         own = pl.pallas_call(
             pack_kernel,
-            out_shape=(piece, piece),
+            out_shape=tuple(pieces),
             in_specs=[vmem] * 2,
             out_specs=(vmem, vmem),
             compiler_params=params,
@@ -166,7 +170,7 @@
         for i in (0, 1):
             passed = pl.pallas_call(
                 choose_kernel,
-                out_shape=(piece, piece),
+                out_shape=(pieces[i], pieces[i]),
                 in_specs=[vmem] * 3,
                 out_specs=(vmem, vmem),
                 compiler_params=params,
@@ -174,9 +178,9 @@
             )(own[i], *got[i])
             came.append([lax.ppermute(passed[k], axes, pairs(2 + k)) for k in (0, 1)])
         near = [own[0], own[1], got[0][0], got[1][0], got[0][1], got[1][1]]
-        best = meet_call(meet_kernel, 6, (8, 6 * half), near)
-        best = meet_call(meet_kernel, 2, (8, 8 * half), near + came[0], best)
-        table = meet_call(last_kernel, 2, (n_grp, rows), near + came[0] + came[1], best)
+        best = meet_call(meet_kernel, 6, near)
+        best = meet_call(meet_kernel, 2, near + came[0], best)
+        table = meet_call(last_kernel, 2, near + came[0] + came[1], best)
         given = lax.all_to_all(table, "grp", 0, 0, tiled=True)
         return jnp.max(given, axis=0)
 

time: 56.8 us -> 56.5 us (level)
    ppermute x4, waiting for transfers between devices: 3.48 us -> 1.96 us  [body(): came.append([lax.ppermute(passed[k], axes, pairs(2 + k)) for k in (0, 1)])]
    ppermute x4, waiting for transfers between devices: 3.69 us -> 5.14 us  [body(): lax.ppermute(own[i], axes, pairs(k))]
  transfers between devices with their start and end apart: 8 -> 8, of which waited for: 3 -> 2; matrix products, arithmetic and copies ran while one was open for 0% -> 0% of each run, Pallas kernels for 7% -> 7%
where the time goes in v6:
time: 56.5 us; the launch traced here: 56.1 us
  starting transfers between devices  27.5 us (49%)
  blocking collectives  12.5 us (22%)
  waiting for transfers between devices  7.1 us (13%)
  Pallas kernels  6.49 us (11%)
  local copies, waits for them, and re-layouts  1.89 us (3%)
    ppermute x4, starting transfers between devices, body(): came.append([lax.ppermute(passed[k], axes, pairs(2 + k)) for k in (0, 1)])  14.1 us
    ppermute x4, starting transfers between devices, body(): lax.ppermute(own[i], axes, pairs(k))  13.3 us
    all_to_all x1, blocking collectives, body(): given = lax.all_to_all(table, 'grp', 0, 0, tiled=True)  12.5 us
    pallas_call x3, Pallas kernels, meet_call(): pl.pallas_call(functools.partial(kernel, len(blocks), count), out_shape=j...  5.93 us
    ppermute x4, waiting for transfers between devices, body(): lax.ppermute(own[i], axes, pairs(k))  5.14 us
    ppermute x4, waiting for transfers between devices, body(): came.append([lax.ppermute(passed[k], axes, pairs(2 + k)) for k in (0, 1)])  1.96 us
    unnamed x6, local copies, waits for them, and re-layouts  1.89 us
  transfers between devices with their start and end apart: 8, of which 2 were waited for; matrix products, arithmetic and copies ran while one was open for 0% of the time, Pallas kernels for 7%

profile of v6, /device:TPU:2, one launch (start us, length us, event | category | flops | bytes accessed | tf_op | source)
XLA Modules:
  0.0 56.1 jit_solution(17107200173145593762)
XLA Ops:
  0.0 0.7 %copy-done.1 = s32[128]{0:T(128)S(1)} copy-done((s32[128]{0:T(128)S(1)}, s32[128]{0:T(128)}, u32[]{:S(2)}) %copy-start.1) | copy-done | bytes 536
  0.7 0.0 copy-done.2
  0.7 1.2 %copy-done = bf16[128,4096]{1,0:T(8,128)(2,1)S(1)} copy-done((bf16[128,4096]{1,0:T(8,128)(2,1)S(1)}, bf16[128,4096]{1,0:T(8,128)(2,1)}, u32[]{:S(2)}) %copy-start) | copy-done | bytes 1048600
  1.9 0.4 pack.1
  2.3 3.5 %collective-permute-start = (bf16[80,4224]{1,0:T(8,128)(2,1)S(1)}, bf16[80,4224]{1,0:T(8,128)(2,1)S(1)}, u32[]{:S(2)}, u32[]{:S(2)}) collective-permute-start(bf16[80,4224]{1,0:T(8,128)(2,1)S(1)} %get-tuple-element.11.own.refs_0_), channel_id=1, source_target_pairs={{4,0},{5,1},{3,2},{7,3},{0,4},{1,5},{2,6},{11,7},{9,8},{13,9},{6,1... | collective-permute-start | bytes 2027528 | tf_op jit(solution)/shard_map/ppermute | solution.py:168
  5.8 3.4 %collective-permute-start.2 = (bf16[80,4224]{1,0:T(8,128)(2,1)S(1)}, bf16[80,4224]{1,0:T(8,128)(2,1)S(1)}, u32[]{:S(2)}, u32[]{:S(2)}) collective-permute-start(bf16[80,4224]{1,0:T(8,128)(2,1)S(1)} %get-tuple-element.11.own.refs_0_), channel_id=1, source_target_pairs={{3,0},{0,1},{1,2},{15,3},{8,4},{6,5},{10,6},{4,7},{11,8},{5,9},{14... | collective-permute-start | bytes 2027528 | tf_op jit(solution)/shard_map/ppermute | solution.py:168
  9.2 2.5 %collective-permute-start.1 = (bf16[48,4224]{1,0:T(8,128)(2,1)S(1)}, bf16[48,4224]{1,0:T(8,128)(2,1)S(1)}, u32[]{:S(2)}, u32[]{:S(2)}) collective-permute-start(bf16[48,4224]{1,0:T(8,128)(2,1)S(1)} %get-tuple-element.12.own.refs_1_), channel_id=1, source_target_pairs={{4,0},{5,1},{3,2},{7,3},{0,4},{1,5},{2,6},{11,7},{9,8},{13,9},{6,1... | collective-permute-start | bytes 1216520 | tf_op jit(solution)/shard_map/ppermute | solution.py:168
  11.7 3.9 %collective-permute-start.3 = (bf16[48,4224]{1,0:T(8,128)(2,1)S(1)}, bf16[48,4224]{1,0:T(8,128)(2,1)S(1)}, u32[]{:S(2)}, u32[]{:S(2)}) collective-permute-start(bf16[48,4224]{1,0:T(8,128)(2,1)S(1)} %get-tuple-element.12.own.refs_1_), channel_id=1, source_target_pairs={{3,0},{0,1},{1,2},{15,3},{8,4},{6,5},{10,6},{4,7},{11,8},{5,9},{14... | collective-permute-start | bytes 1216520 | tf_op jit(solution)/shard_map/ppermute | solution.py:168
  15.6 0.0 collective-permute-done.first.refs_2_
  15.7 5.1 %collective-permute-done.2.second.refs_4_ = bf16[80,4224]{1,0:T(8,128)(2,1)S(1)} collective-permute-done((bf16[80,4224]{1,0:T(8,128)(2,1)S(1)}, bf16[80,4224]{1,0:T(8,128)(2,1)S(1)}, u32[]{:S(2)}, u32[]{:S(2)}) %collective-permute-start.2) | collective-permute-done | bytes 675872 | tf_op jit(solution)/shard_map/ppermute | solution.py:168
  20.8 0.1 choose.2
  20.9 1.9 %collective-permute-start.4 = (bf16[80,4224]{1,0:T(8,128)(2,1)S(1)}, bf16[80,4224]{1,0:T(8,128)(2,1)S(1)}, u32[]{:S(2)}, u32[]{:S(2)}) collective-permute-start(bf16[80,4224]{1,0:T(8,128)(2,1)S(1)} %get-tuple-element.13), channel_id=1, source_target_pairs={{3,0},{13,1},{1,2},{15,3},{8,4},{6,5},{7,6},{4,7},{11,8},{5,9},{9,... | collective-permute-start | bytes 2027528 | tf_op jit(solution)/shard_map/ppermute | solution.py:179
  22.8 5.1 %collective-permute-start.5 = (bf16[80,4224]{1,0:T(8,128)(2,1)S(1)}, bf16[80,4224]{1,0:T(8,128)(2,1)S(1)}, u32[]{:S(2)}, u32[]{:S(2)}) collective-permute-start(bf16[80,4224]{1,0:T(8,128)(2,1)S(1)} %get-tuple-element.14), channel_id=1, source_target_pairs={{12,0},{0,1},{3,2},{7,3},{5,4},{4,5},{2,6},{6,7},{9,8},{10,9},{14,... | collective-permute-start | bytes 2027528 | tf_op jit(solution)/shard_map/ppermute | solution.py:179
  28.0 0.0 collective-permute-done.3.second.refs_5_
  28.0 0.1 choose.3
  28.1 1.9 %collective-permute-start.6 = (bf16[48,4224]{1,0:T(8,128)(2,1)S(1)}, bf16[48,4224]{1,0:T(8,128)(2,1)S(1)}, u32[]{:S(2)}, u32[]{:S(2)}) collective-permute-start(bf16[48,4224]{1,0:T(8,128)(2,1)S(1)} %get-tuple-element.15), channel_id=1, source_target_pairs={{3,0},{13,1},{1,2},{15,3},{8,4},{6,5},{7,6},{4,7},{11,8},{5,9},{9,... | collective-permute-start | bytes 1216520 | tf_op jit(solution)/shard_map/ppermute | solution.py:179
  30.0 5.1 %collective-permute-start.7 = (bf16[48,4224]{1,0:T(8,128)(2,1)S(1)}, bf16[48,4224]{1,0:T(8,128)(2,1)S(1)}, u32[]{:S(2)}, u32[]{:S(2)}) collective-permute-start(bf16[48,4224]{1,0:T(8,128)(2,1)S(1)} %get-tuple-element.16), channel_id=1, source_target_pairs={{12,0},{0,1},{3,2},{7,3},{5,4},{4,5},{2,6},{6,7},{9,8},{10,9},{14,... | collective-permute-start | bytes 1216520 | tf_op jit(solution)/shard_map/ppermute | solution.py:179
  35.2 2.0 %meet_kernel.2.refs_8_ = f32[8,384]{1,0:T(8,128)S(1)} custom-call(bf16[80,4224]{1,0:T(8,128)(2,1)S(1)} %get-tuple-element.11.own.refs_0_, bf16[48,4224]{1,0:T(8,128)(2,1)S(1)} %get-tuple-element.12.own.refs_1_, bf16[80,4224]{1,0:T(8,128)(2,1)S(1)} %collective-permute-done.first.refs_2_, bf16[48,4224]{1,0:T(8,128)(2,1)S(1)} %collective-permute-done.1.first.refs_3_, ...), custom_call_target="tpu_custom_call" | custom-call | flops 1207959552 | bytes 3145728 | tf_op jit(solution)/shard_map/meet_kernel/pallas_call | solution.py:150
  37.2 1.9 %meet_kernel.3.refs_10_ = f32[8,544]{1,0:T(8,128)S(1)} custom-call(bf16[80,4224]{1,0:T(8,128)(2,1)S(1)} %get-tuple-element.11.own.refs_0_, bf16[48,4224]{1,0:T(8,128)(2,1)S(1)} %get-tuple-element.12.own.refs_1_, bf16[80,4224]{1,0:T(8,128)(2,1)S(1)} %collective-permute-done.first.refs_2_, bf16[48,4224]{1,0:T(8,128)(2,1)S(1)} %collective-permute-done.1.first.refs_3_, ...), custom_call_target="tpu_custom_call" | custom-call | flops 713031680 | bytes 4456448 | tf_op jit(solution)/shard_map/meet_kernel/pallas_call | solution.py:150
  39.1 0.0 collective-permute-done.6.refs_8_
  39.2 1.9 %collective-permute-done.7.refs_9_ = bf16[48,4224]{1,0:T(8,128)(2,1)S(1)} collective-permute-done((bf16[48,4224]{1,0:T(8,128)(2,1)S(1)}, bf16[48,4224]{1,0:T(8,128)(2,1)S(1)}, u32[]{:S(2)}, u32[]{:S(2)}) %collective-permute-start.7) | collective-permute-done | bytes 405536 | tf_op jit(solution)/shard_map/ppermute | solution.py:179
  41.1 2.0 %last_kernel.1 = f32[16,128]{1,0:T(8,128)S(1)} custom-call(bf16[80,4224]{1,0:T(8,128)(2,1)S(1)} %get-tuple-element.11.own.refs_0_, bf16[48,4224]{1,0:T(8,128)(2,1)S(1)} %get-tuple-element.12.own.refs_1_, bf16[80,4224]{1,0:T(8,128)(2,1)S(1)} %collective-permute-done.first.refs_2_, bf16[48,4224]{1,0:T(8,128)(2,1)S(1)} %collective-permute-done.1.first.refs_3_, ...), custom_call_target="tpu_custom_call" | custom-call | flops 503316480 | bytes 5242880 | tf_op jit(solution)/shard_map/last_kernel/pallas_call | solution.py:150
  43.1 12.5 %all_to_all.9 = f32[16,1,128]{2,1,0:T(1,128)S(1)} all-to-all(f32[16,1,128]{2,1,0:T(1,128)S(1)} %bitcast.5), channel_id=1, replica_groups=mesh['shard'=32,'grp'=16] {'grp'}, dimensions={0} | all-to-all | bytes 16384 | tf_op jit(solution)/shard_map/all_to_all | solution.py:184
  55.6 0.5 reduce_max.9
  (7 shorter events, 0.0 us)
Async XLA Ops:
  0.0 0.7 %copy-start.1 = (s32[128]{0:T(128)S(1)}, s32[128]{0:T(128)}, u32[]{:S(2)}) copy-start(s32[128]{0:T(128)} %param.5) | copy-start | bytes 1540
  0.0 0.7 %copy-start.2 = (s32[128]{0:T(128)S(1)}, s32[128]{0:T(128)}, u32[]{:S(2)}) copy-start(s32[128]{0:T(128)} %param.4) | copy-start | bytes 1540
  0.7 1.2 %copy-start = (bf16[128,4096]{1,0:T(8,128)(2,1)S(1)}, bf16[128,4096]{1,0:T(8,128)(2,1)}, u32[]{:S(2)}) copy-start(bf16[128,4096]{1,0:T(8,128)(2,1)} %emb.1) | copy-start | bytes 3145732
  2.3 13.4 %collective-permute-start = (bf16[80,4224]{1,0:T(8,128)(2,1)S(1)}, bf16[80,4224]{1,0:T(8,128)(2,1)S(1)}, u32[]{:S(2)}, u32[]{:S(2)}) collective-permute-start(bf16[80,4224]{1,0:T(8,128)(2,1)S(1)} %get-tuple-element.11.own.refs_0_), channel_id=1, source_target_pairs={{4,0},{5,1},{3,2},{7,3},{0,4},{1,5},{2,6},{11,7},{9,8},{13,9},{6,1... | collective-permute-start | bytes 2027528 | tf_op jit(solution)/shard_map/ppermute | solution.py:168
  5.8 15.0 %collective-permute-start.2 = (bf16[80,4224]{1,0:T(8,128)(2,1)S(1)}, bf16[80,4224]{1,0:T(8,128)(2,1)S(1)}, u32[]{:S(2)}, u32[]{:S(2)}) collective-permute-start(bf16[80,4224]{1,0:T(8,128)(2,1)S(1)} %get-tuple-element.11.own.refs_0_), channel_id=1, source_target_pairs={{3,0},{0,1},{1,2},{15,3},{8,4},{6,5},{10,6},{4,7},{11,8},{5,9},{14... | collective-permute-start | bytes 2027528 | tf_op jit(solution)/shard_map/ppermute | solution.py:168
  9.2 18.8 %collective-permute-start.1 = (bf16[48,4224]{1,0:T(8,128)(2,1)S(1)}, bf16[48,4224]{1,0:T(8,128)(2,1)S(1)}, u32[]{:S(2)}, u32[]{:S(2)}) collective-permute-start(bf16[48,4224]{1,0:T(8,128)(2,1)S(1)} %get-tuple-element.12.own.refs_1_), channel_id=1, source_target_pairs={{4,0},{5,1},{3,2},{7,3},{0,4},{1,5},{2,6},{11,7},{9,8},{13,9},{6,1... | collective-permute-start | bytes 1216520 | tf_op jit(solution)/shard_map/ppermute | solution.py:168
  11.7 16.3 %collective-permute-start.3 = (bf16[48,4224]{1,0:T(8,128)(2,1)S(1)}, bf16[48,4224]{1,0:T(8,128)(2,1)S(1)}, u32[]{:S(2)}, u32[]{:S(2)}) collective-permute-start(bf16[48,4224]{1,0:T(8,128)(2,1)S(1)} %get-tuple-element.12.own.refs_1_), channel_id=1, source_target_pairs={{3,0},{0,1},{1,2},{15,3},{8,4},{6,5},{10,6},{4,7},{11,8},{5,9},{14... | collective-permute-start | bytes 1216520 | tf_op jit(solution)/shard_map/ppermute | solution.py:168
  20.9 16.3 %collective-permute-start.4 = (bf16[80,4224]{1,0:T(8,128)(2,1)S(1)}, bf16[80,4224]{1,0:T(8,128)(2,1)S(1)}, u32[]{:S(2)}, u32[]{:S(2)}) collective-permute-start(bf16[80,4224]{1,0:T(8,128)(2,1)S(1)} %get-tuple-element.13), channel_id=1, source_target_pairs={{3,0},{13,1},{1,2},{15,3},{8,4},{6,5},{7,6},{4,7},{11,8},{5,9},{9,... | collective-permute-start | bytes 2027528 | tf_op jit(solution)/shard_map/ppermute | solution.py:179
  22.8 14.3 %collective-permute-start.5 = (bf16[80,4224]{1,0:T(8,128)(2,1)S(1)}, bf16[80,4224]{1,0:T(8,128)(2,1)S(1)}, u32[]{:S(2)}, u32[]{:S(2)}) collective-permute-start(bf16[80,4224]{1,0:T(8,128)(2,1)S(1)} %get-tuple-element.14), channel_id=1, source_target_pairs={{12,0},{0,1},{3,2},{7,3},{5,4},{4,5},{2,6},{6,7},{9,8},{10,9},{14,... | collective-permute-start | bytes 2027528 | tf_op jit(solution)/shard_map/ppermute | solution.py:179
  28.1 11.1 %collective-permute-start.6 = (bf16[48,4224]{1,0:T(8,128)(2,1)S(1)}, bf16[48,4224]{1,0:T(8,128)(2,1)S(1)}, u32[]{:S(2)}, u32[]{:S(2)}) collective-permute-start(bf16[48,4224]{1,0:T(8,128)(2,1)S(1)} %get-tuple-element.15), channel_id=1, source_target_pairs={{3,0},{13,1},{1,2},{15,3},{8,4},{6,5},{7,6},{4,7},{11,8},{5,9},{9,... | collective-permute-start | bytes 1216520 | tf_op jit(solution)/shard_map/ppermute | solution.py:179
  30.0 11.1 %collective-permute-start.7 = (bf16[48,4224]{1,0:T(8,128)(2,1)S(1)}, bf16[48,4224]{1,0:T(8,128)(2,1)S(1)}, u32[]{:S(2)}, u32[]{:S(2)}) collective-permute-start(bf16[48,4224]{1,0:T(8,128)(2,1)S(1)} %get-tuple-element.16), channel_id=1, source_target_pairs={{12,0},{0,1},{3,2},{7,3},{5,4},{4,5},{2,6},{6,7},{9,8},{10,9},{14,... | collective-permute-start | bytes 1216520 | tf_op jit(solution)/shard_map/ppermute | solution.py:179
